TPU v7x, 1024 devices: a whole 8x8x8 slice. The times are simulated.
1024 devices in a mesh: dp: 128 (over x, y, core), tp: 8 (over z).
Axes of the slice: x: 8, y: 8, z: 8, core: 2. Of those that a mesh axis runs over, the one named last changes fastest.
Arguments:
- normed: bfloat16 [128, 768, 4096], P('dp', 'tp'), may hold values from -6 to 6
- key_grad: bfloat16 [128, 768, 1024], P('dp', None, 'tp'), may hold values from -0.18 to 0.18
- error_in: bfloat16 [128, 4096, 1024], P('dp', None, 'tp'), may hold values from -3 to 3
- q_init: float32 [1024, 32], P('tp'), may hold values from -6 to 6
Outputs:
- error_next: bfloat16 [128, 4096, 1024], P('dp', None, 'tp')
- p_basis: float32 [4096, 32], replicated
- q_mean: float32 [1024, 32], P('tp')
All inputs are finite; a program needn't handle non-finite values.
Results may differ from a plain program's by a relative error of at most 0.007.
Values may be sent and summed in bfloat16 or wider, within the bound.
No kernel may reach another device: no remote copies, remote signals or barrier semaphores. Data moves between devices by JAX's collectives and lax.ppermute only.
A program may use at most 32 MiB of HBM per device.

v0:
```python
import jax
import jax.numpy as jnp
from jax import lax
from jax.sharding import PartitionSpec as P


def accumulate(piece, key_rows):
    return lax.dot_general(
        piece, key_rows, (((0,), (0,)), ((), ())), preferred_element_type=jnp.float32
    )


def on_device(normed, key_grad, error_in, q_init):
    high = lax.Precision.HIGHEST
    inputs = normed[0]
    grads = key_grad[0]
    errors = error_in[0].astype(jnp.float32)
    grad = accumulate(lax.all_gather(inputs, "tp", axis=0, tiled=True), grads)
    merged = grad + errors
    p_local = jnp.dot(merged, q_init, precision=high)
    p_sum = lax.psum(p_local, ("dp", "tp"))
    gram = jnp.dot(p_sum.T, p_sum, precision=high)
    lower = jnp.linalg.cholesky(gram)
    p_basis = lax.linalg.triangular_solve(
        lower, p_sum, left_side=False, lower=True, transpose_a=True
    )
    q_local = lax.dot_general(merged, p_basis, (((0,), (0,)), ((), ())), precision=high)
    q_mean = lax.psum(q_local, "dp") / lax.axis_size("dp")
    approx = jnp.dot(p_basis, q_mean.T, precision=high)
    error_next = (merged - approx).astype(jnp.bfloat16)[None]
    return (error_next, p_basis, q_mean)


def solution(mesh):
    placed = (P("dp", "tp", None), P("dp", None, "tp"), P("dp", None, "tp"), P("tp", None))
    return jax.shard_map(
        on_device,
        mesh=mesh,
        in_specs=placed,
        out_specs=(P("dp", None, "tp"), P(), P("tp", None)),
        check_vma=False,
    )
```

profile of v0, /device:TPU:1, one launch (start us, length us, event | category | flops | bytes accessed | tf_op | source)
XLA Modules:
  0.0 905.9 jit_solution(8645751908250957817)
XLA Ops:
  7.2 0.0 copy-start
  7.2 0.0 all-gather.3.cloned.1.call-start
  7.2 0.7 all-gather.3.cloned.1.call-update
  7.9 0.0 copy-start.3
  7.9 0.0 all-reduce.2.cloned.1.call-start
  8.0 96.7 %all-gather.3.cloned.1.call-done = bf16[1,768,4096]{2,1,0:T(8,128)(2,1)} async-done(((bf16[1,96,4096]{2,1,0:T(8,128)(2,1)}), bf16[1,768,4096]{2,1,0:T(8,128)(2,1)}) %all-gather.3.cloned.1.call-update) | async-done | bytes 6291472 | tf_op jit(solution)/shard_map/all_gather | solution.py:18
  104.7 0.0 copy-done
  104.7 4.9 fusion.2
  109.6 0.0 copy-done.3
  109.6 3.0 fusion.12
  112.6 0.0 all-reduce.2.cloned.1.call-update
  112.6 284.4 %all-reduce.2.cloned.1.call-done = f32[4096,32]{0,1:T(8,128)} async-done(((f32[4096,32]{0,1:T(8,128)}), f32[4096,32]{0,1:T(8,128)}) %all-reduce.2.cloned.1.call-update) | async-done | bytes 524304 | tf_op jit(solution)/shard_map/psum | solution.py:21
  397.0 1.8 fusion.13
  398.7 0.1 copy.7
  398.8 2.9 cholesky.16
  401.8 0.6 compare_reduce_fusion
  402.4 0.7 fusion.8
  403.1 2.4 custom-call.6
  405.5 1.7 fusion.9
  407.2 0.0 copy-start.1
  407.2 1.3 fusion.14
  408.5 486.1 %psum.15 = f32[128,32]{0,1:T(8,128)S(1)} all-reduce(f32[128,32]{0,1:T(8,128)S(1)} %fusion.14), channel_id=1, replica_groups=mesh['dp'=128,'tp'=8] {'dp'}, use_global_device_ids=true, to_apply=%region_3.4 | all-reduce | flops 4096 | bytes 32768 | tf_op jit(solution)/shard_map/psum | solution.py:28
  894.6 0.0 copy-start.2
  894.6 4.4 fusion.6
  899.1 0.0 copy-done.1
  899.1 0.0 copy-done.2
  (3 shorter events, 0.0 us)
Async XLA Ops:
  7.2 97.5 %copy-start = (bf16[1,768,128]{2,1,0:T(8,128)(2,1)S(1)}, bf16[1,768,128]{2,1,0:T(8,128)(2,1)}, u32[]{:S(2)}) copy-start(bf16[1,768,128]{2,1,0:T(8,128)(2,1)} %param.5) | copy-start | bytes 589828
  7.2 97.5 %all-gather.3.cloned.1.call-start = ((), (), s32[]{:S(2)}) async-start(), calls=%async_computation.1 | async-start | bytes 7077888 | tf_op jit(solution)/shard_map/all_gather | solution.py:18
  7.9 101.7 %copy-start.3 = (f32[128,32]{0,1:T(8,128)S(1)}, f32[128,32]{0,1:T(8,128)}, u32[]{:S(2)}) copy-start(f32[128,32]{0,1:T(8,128)} %param.7) | copy-start | bytes 49156
  7.9 389.0 %all-reduce.2.cloned.1.call-start = ((), (), s32[]{:S(2)}) async-start(), calls=%async_computation | async-start | bytes 1048576 | tf_op jit(solution)/shard_map/psum | solution.py:21
  407.2 491.9 %copy-start.1 = (f32[4096,32]{0,1:T(8,128)}, f32[4096,32]{0,1:T(8,128)S(1)}, u32[]{:S(2)}) copy-start(f32[4096,32]{0,1:T(8,128)S(1)} %fusion.9) | copy-start | bytes 1572868
  894.6 4.4 copy-start.2
Sparse Core Ops, SparseCore 0:
  10.7 93.9 all-gather.2
  112.7 284.2 all-reduce.1
where the time goes:
time: 910 us; the launch traced here: 906 us
  blocking collectives  486 us (53%)
  waiting for transfers between devices  382 us (42%)
  matrix products  17 us (2%)
  between operations  14.1 us (2%)
    psum x1, blocking collectives, on_device(): q_mean = lax.psum(q_local, 'dp') / lax.axis_size('dp')  486 us
    psum x1, waiting for transfers between devices, on_device(): p_sum = lax.psum(p_local, ('dp', 'tp'))  284 us
    all_gather x1, waiting for transfers between devices, on_device(): grad = accumulate(lax.all_gather(inputs, 'tp', axis=0, tiled=True), grads)  96.7 us
  transfers between devices with their start and end apart: 2, of which 2 were waited for; matrix products, arithmetic and copies ran while one was open for 0% of the time, Pallas kernels for 0%

commit v1 on v0

v1 whole, which is shorter than its diff:
```python
import math

import jax
import jax.numpy as jnp
from jax import lax
from jax.sharding import Mesh, PartitionSpec as P

F32 = jnp.float32
BF16 = jnp.bfloat16
HIGH = lax.Precision.HIGHEST
PLANE = ("x", "y")


def two_terms(value):
    head = lax.reduce_precision(value, 8, 7)
    return jnp.concatenate([head.astype(BF16), (value - head).astype(BF16)], axis=0)


def fold(value):
    half = value.shape[0] // 2
    return value[:half] + value[half:]


def swap(value, axes):
    return lax.all_to_all(value, axes, 0, 0, tiled=True)


def spread(value, axes):
    return swap(jnp.broadcast_to(value[None], (lax.axis_size(axes),) + value.shape), axes)


def on_device(normed, key_grad, error_in, q_init):
    inputs, grads, errors = normed[0], key_grad[0], error_in[0]
    tp = lax.axis_size("z")
    plane = lax.axis_size(PLANE)
    replicas = plane * lax.axis_size("c")
    tokens, wide = inputs.shape
    rank = q_init.shape[1]
    gathered = lax.all_gather(inputs, "z", axis=0, tiled=True)

    q_terms = two_terms(q_init.T)
    by_head = fold(lax.dot_general(q_terms, grads, (((1,), (1,)), ((), ())), preferred_element_type=F32))
    by_token = jnp.transpose(by_head.reshape(rank, tp, tokens), (1, 0, 2))
    mine = jnp.sum(swap(by_token, "z"), axis=0)

    p_local = jnp.dot(two_terms(mine), inputs, preferred_element_type=F32)
    p_local += lax.dot_general(q_terms, errors, (((1,), (1,)), ((), ())), preferred_element_type=F32)
    p_local = fold(p_local)
    lanes = 128
    columns = wide // lanes
    halves = plane // columns
    depth = rank // halves
    pieces = jnp.transpose(p_local.reshape(halves, depth, columns, lanes), (0, 2, 1, 3))
    pieces = pieces.reshape(plane, depth, lanes).astype(BF16)
    piece = jnp.sum(swap(pieces, PLANE).astype(F32), axis=0)
    piece = jnp.sum(spread(piece, ("c", "z")), axis=0)
    p_sum = spread(piece, PLANE).reshape(halves, columns, depth, lanes)
    p_sum = jnp.transpose(p_sum, (0, 2, 1, 3)).reshape(rank, wide)

    gram = lax.dot_general(p_sum, p_sum, (((1,), (1,)), ((), ())), precision=HIGH)
    lower = jnp.linalg.cholesky(gram)
    inverse = lax.linalg.triangular_solve(lower, jnp.eye(rank, dtype=F32), left_side=True, lower=True)
    p_basis = jnp.dot(inverse, p_sum, precision=HIGH)

    merged = lax.dot_general(gathered, grads, (((0,), (0,)), ((), ())), preferred_element_type=F32)
    merged = merged + errors.astype(F32)
    q_local = jnp.dot(p_basis, merged, precision=HIGH)
    q_local = q_local + lax.ppermute(q_local, "c", [(0, 1), (1, 0)])
    q_mean = jnp.sum(spread(q_local.astype(BF16), PLANE).astype(F32), axis=0) / replicas
    approx = lax.dot_general(p_basis, q_mean, (((0,), (0,)), ((), ())), precision=HIGH)
    error_next = (merged - approx).astype(BF16)[None]
    return (error_next, p_basis.T, q_mean.T)


def solution(mesh):
    side = math.isqrt(mesh.shape["dp"] // 2)
    whole = Mesh(mesh.devices.reshape(side, side, 2, mesh.shape["tp"]), ("x", "y", "c", "z"))
    dp = ("x", "y", "c")
    placed = (P(dp, "z", None), P(dp, None, "z"), P(dp, None, "z"), P("z", None))
    return jax.shard_map(
        on_device,
        mesh=whole,
        in_specs=placed,
        out_specs=(P(dp, None, "z"), P(), P("z", None)),
        check_vma=False,
    )
```

time: 910 us -> 160 us (0.18)
  waiting for transfers between devices: 382 us -> 3.32 us
  blocking collectives: 486 us -> 115 us
    psum x1 -> x0, blocking collectives: 486 us -> none  [on_device(): q_mean = lax.psum(q_local, 'dp') / lax.axis_size('dp')]
    psum x1 -> x0, waiting for transfers between devices: 284 us -> none  [on_device(): p_sum = lax.psum(p_local, ('dp', 'tp'))]
    all_to_all x0 -> x5, blocking collectives: none -> 115 us  [swap(): return lax.all_to_all(value, axes, 0, 0, tiled=True)]
    all_gather x1, waiting for transfers between devices: 96.7 us -> 1.82 us  [on_device(): gathered = lax.all_gather(inputs, 'z', axis=0, tiled=True)]
  transfers between devices with their start and end apart: 2 -> 2, of which waited for: 2 -> 2; matrix products, arithmetic and copies ran while one was open for 0% -> 7% of each run, Pallas kernels for 0% -> 0%
where the time goes in v1:
time: 160 us; the launch traced here: 158 us
  blocking collectives  115 us (72%)
  between operations  14.2 us (9%)
  matrix products  13.2 us (8%)
  other arithmetic  8.34 us (5%)
  waiting for transfers between devices  3.32 us (2%)
  starting transfers between devices  2.94 us (2%)
    all_to_all x5, blocking collectives, swap(): return lax.all_to_all(value, axes, 0, 0, tiled=True)  115 us
    dot_general x1, matrix products, on_device(): lax.dot_general(gathered, grads, (((0,), (0,)), ((), ())), preferred_elem...  4.68 us
    dot_general x1, matrix products, on_device(): lax.dot_general(p_basis, q_mean, (((0,), (0,)), ((), ())), precision=HIGH)  4.43 us
    another operation x3, other arithmetic, on_device(): lower = jnp.linalg.cholesky(gram)  3.6 us
  transfers between devices with their start and end apart: 2, of which 2 were waited for; matrix products, arithmetic and copies ran while one was open for 7% of the time, Pallas kernels for 0%

profile of v1, /device:TPU:1, one launch (start us, length us, event | category | flops | bytes accessed | tf_op | source)
XLA Modules:
  0.0 157.9 jit_solution(4209159740486830552)
XLA Ops:
  7.2 0.7 all-gather.3.cloned.1.call-update
  7.9 0.7 reduce-precision_convert_fusion.1
  8.7 0.2 fusion.18
  8.9 0.1 reshape.31
  9.0 24.8 %all_to_all.25 = f32[8,32,96]{2,1,0:T(8,128)S(1)} all-to-all(f32[8,32,96]{2,1,0:T(8,128)S(1)} %bitcast.64), channel_id=1, replica_groups=mesh['x'=8,'y'=8,'c'=2,'z'=8] {'z'}, dimensions={0} | all-to-all | bytes 196608 | tf_op jit(solution)/shard_map/all_to_all | solution.py:25
  33.9 0.3 fusion.8
  34.2 0.5 convolution_add_fusion
  34.7 0.1 fusion.17
  34.8 0.1 copy.18
  34.9 25.5 %all_to_all.26 = bf16[64,16,128]{2,1,0:T(8,128)(2,1)S(1)} all-to-all(bf16[64,16,128]{2,1,0:T(8,128)(2,1)S(1)} %bitcast.63), channel_id=1, replica_groups=mesh['x'=8,'y'=8,'c'=2,'z'=8] {'x','y'}, dimensions={0} | all-to-all | bytes 524288 | tf_op jit(solution)/shard_map/all_to_all | solution.py:25
  60.4 0.1 convert_reduce_fusion.1
  60.4 15.3 %all_to_all.27 = f32[16,16,128]{2,1,0:T(8,128)S(1)} all-to-all(f32[16,16,128]{2,1,0:T(8,128)S(1)} %broadcast_in_dim.10), channel_id=1, replica_groups=mesh['x'=8,'y'=8,'c'=2,'z'=8] {'c','z'}, dimensions={0} | all-to-all | bytes 262144 | tf_op jit(solution)/shard_map/all_to_all | solution.py:25
  75.8 21.0 %all_to_all.28 = f32[64,16,128]{2,1,0:T(8,128)S(1)} all-to-all(f32[64,16,128]{2,1,0:T(8,128)S(1)} %broadcast_in_dim.11), channel_id=1, replica_groups=mesh['x'=8,'y'=8,'c'=2,'z'=8] {'x','y'}, dimensions={0} | all-to-all | bytes 1048576 | tf_op jit(solution)/shard_map/all_to_all | solution.py:25
  96.8 0.2 copy.19
  97.0 0.8 fusion.12
  97.8 0.1 copy.20
  97.9 2.9 %cholesky.17 = f32[32,32]{1,0:T(8,128)S(1)} custom-call(f32[32,32]{1,0:T(8,128)S(1)} %fusion.29), custom_call_target="Cholesky" | custom-call | tf_op jit(solution)/shard_map/jit(cholesky)/cholesky | solution.py:61
  100.8 0.6 compare_reduce_fusion
  101.5 0.7 fusion.21
  102.1 2.5 %custom-call.6 = f32[1,32,32]{1,2,0:T(8,128)S(1)} custom-call(f32[1,32,32]{2,1,0:T(8,128)S(1)} %fusion.21), custom_call_target="InvertDiagBlocksLowerTriangular" | custom-call | tf_op jit(solution)/shard_map/triangular_solve | solution.py:62
  104.6 0.2 fusion.27
  104.8 0.9 fusion.10
  105.7 1.8 %all-gather.3.cloned.1.call-done = bf16[1,768,4096]{2,1,0:T(8,128)(2,1)} async-done(((bf16[1,96,4096]{2,1,0:T(8,128)(2,1)}), bf16[1,768,4096]{2,1,0:T(8,128)(2,1)}) %all-gather.3.cloned.1.call-update) | async-done | bytes 6291472 | tf_op jit(solution)/shard_map/all_gather | solution.py:39
  107.5 4.7 %fusion.2 = f32[4096,128]{1,0:T(8,128)S(1)} fusion(bf16[1,768,4096]{2,1,0:T(8,128)(2,1)} %all-gather.3.cloned.1.call-done, bf16[1,4096,128]{2,1,0:T(8,128)(2,1)S(1)} %copy-done.2, bf16[1,768,128]{2,1,0:T(8,128)(2,1)S(1)} %copy-done), kind=kOutput, calls=%fused_computation.3 | convolution fusion | flops 806354944 | bytes 9633792 | tf_op jit(solution)/shard_map/dot_general | solution.py:65
  112.2 1.2 fusion.36
  113.4 2.9 %collective-permute-start = (f32[32,128]{1,0:T(8,128)S(1)}, f32[32,128]{1,0:T(8,128)S(1)}, u32[]{:S(2)}, u32[]{:S(2)}) collective-permute-start(f32[32,128]{1,0:T(8,128)S(1)} %fusion.36), channel_id=1, source_target_pairs={{0,8},{8,0},{1,9},{9,1},{2,10},{10,2},{3,11},{11,3},{4,12},{12,4},... | collective-permute-start | bytes 49160 | tf_op jit(solution)/shard_map/ppermute | solution.py:68
  116.3 0.8 collective-permute-done
  117.1 0.1 broadcast_in_dim.12
  117.2 28.7 %all_to_all.29 = bf16[64,32,128]{2,1,0:T(8,128)(2,1)S(1)} all-to-all(bf16[64,32,128]{2,1,0:T(8,128)(2,1)S(1)} %broadcast_in_dim.12), channel_id=1, replica_groups=mesh['x'=8,'y'=8,'c'=2,'z'=8] {'x','y'}, dimensions={0} | all-to-all | bytes 1048576 | tf_op jit(solution)/shard_map/all_to_all | solution.py:25
  145.9 0.1 convert_reduce_fusion
  146.0 4.4 %fusion.6 = bf16[1,4096,128]{2,1,0:T(8,128)(2,1)} fusion(f32[4096,128]{1,0:T(8,128)S(1)} %fusion.2, f32[32,4096]{1,0:T(8,128)S(1)} %fusion.10, f32[32,128]{1,0:T(8,128)S(1)} %convert_reduce_fusion), kind=kOutput, calls=%fused_computation.6 | convolution fusion | flops 202379264 | bytes 3686400 | tf_op jit(solution)/shard_map/dot_general | solution.py:70
  150.4 0.6 multiply_bitcast_fusion
  (20 shorter events, 0.3 us)
Async XLA Ops:
  7.2 1.5 copy-start
  7.2 26.7 %copy-start.3 = (bf16[1,96,4096]{2,1,0:T(8,128)(2,1)S(1)}, bf16[1,96,4096]{2,1,0:T(8,128)(2,1)}, u32[]{:S(2)}) copy-start(bf16[1,96,4096]{2,1,0:T(8,128)(2,1)} %param.4) | copy-start | bytes 2359300
  7.2 27.0 %copy-start.2 = (bf16[1,4096,128]{2,1,0:T(8,128)(2,1)S(1)}, bf16[1,4096,128]{2,1,0:T(8,128)(2,1)}, u32[]{:S(2)}) copy-start(bf16[1,4096,128]{2,1,0:T(8,128)(2,1)} %param.6) | copy-start | bytes 3145732
  7.2 100.3 %all-gather.3.cloned.1.call-start = ((), (), s32[]{:S(2)}) async-start(), calls=%async_computation.5 | async-start | bytes 7077888 | tf_op jit(solution)/shard_map/all_gather | solution.py:39
  105.7 40.3 %copy-start.1 = (f32[32,4096]{1,0:T(8,128)}, f32[32,4096]{1,0:T(8,128)S(1)}, u32[]{:S(2)}) copy-start(f32[32,4096]{1,0:T(8,128)S(1)} %fusion.10) | copy-start | bytes 1572868
  113.4 3.7 %collective-permute-start = (f32[32,128]{1,0:T(8,128)S(1)}, f32[32,128]{1,0:T(8,128)S(1)}, u32[]{:S(2)}, u32[]{:S(2)}) collective-permute-start(f32[32,128]{1,0:T(8,128)S(1)} %fusion.36), channel_id=1, source_target_pairs={{0,8},{8,0},{1,9},{9,1},{2,10},{10,2},{3,11},{11,3},{4,12},{12,4},... | collective-permute-start | bytes 49160 | tf_op jit(solution)/shard_map/ppermute | solution.py:68
Sparse Core Ops, SparseCore 0:
  10.7 96.7 all-gather.2

commit v2 on v1

--- a/solution.py
+++ b/solution.py
@@ -1,14 +1,20 @@
+import functools
 import math
 
 import jax
 import jax.numpy as jnp
 from jax import lax
+from jax.experimental import pallas as pl
+from jax.experimental.pallas import tpu as pltpu
 from jax.sharding import Mesh, PartitionSpec as P
 
 F32 = jnp.float32
 BF16 = jnp.bfloat16
 HIGH = lax.Precision.HIGHEST
 PLANE = ("x", "y")
+ROWS = ((1,), (1,))
+COLUMNS = ((0,), (0,))
+PLAIN = ((1,), (0,))
 
 
 def two_terms(value):
@@ -27,6 +33,100 @@
 
 def spread(value, axes):
     return swap(jnp.broadcast_to(value[None], (lax.axis_size(axes),) + value.shape), axes)
+
+
+def dot(a, b, axes=PLAIN):
+    return lax.dot_general(a, b, (axes, ((), ())), preferred_element_type=F32)
+
+
+def split(value):
+    head = value.astype(BF16)
+    return head, (value - head.astype(F32)).astype(BF16)
+
+
+def merge_body(inputs, grads, errors, basis, merged, q_out, turned):
+    @pl.when(pl.program_id(0) == 0)
+    def _():
+        q_out[...] = jnp.zeros_like(q_out)
+        turned[...] = grads[...].T
+
+    block = dot(turned[...], inputs[...]).T + errors[...].astype(F32)
+    merged[...] = block
+    high, low = split(block)
+    b_high, b_low = split(basis[...])
+    rank = b_high.shape[0]
+    q = dot(jnp.concatenate([b_high, b_low], axis=0), high)
+    q_out[...] += q[:rank] + q[rank:] + dot(b_high, low)
+
+
+def merge(inputs, grads, errors, basis, block):
+    tokens, wide = inputs.shape
+    cols, rank = grads.shape[1], basis.shape[0]
+    return pl.pallas_call(
+        merge_body,
+        grid=(wide // block,),
+        in_specs=[
+            pl.BlockSpec((tokens, block), lambda i: (0, i)),
+            pl.BlockSpec((tokens, cols), lambda i: (0, 0)),
+            pl.BlockSpec((block, cols), lambda i: (i, 0)),
+            pl.BlockSpec((rank, block), lambda i: (0, i)),
+        ],
+        out_specs=[
+            pl.BlockSpec((block, cols), lambda i: (i, 0)),
+            pl.BlockSpec((rank, cols), lambda i: (0, 0)),
+        ],
+        out_shape=[
+            jax.ShapeDtypeStruct((wide, cols), F32),
+            jax.ShapeDtypeStruct((rank, cols), F32),
+        ],
+        scratch_shapes=[pltpu.VMEM((cols, tokens), BF16)],
+        compiler_params=pltpu.CompilerParams(vmem_limit_bytes=52 * 2**20),
+        cost_estimate=pl.CostEstimate(
+            flops=2 * tokens * wide * cols, bytes_accessed=2 * tokens * wide, transcendentals=0
+        ),
+        name="merge",
+    )(inputs, grads, errors, basis)
+
+
+def finish_body(scale, merged, basis, terms, error_next, q_mean, factors):
+    @pl.when(pl.program_id(0) == 0)
+    def _():
+        mean = jnp.sum(terms[...], axis=0) * scale
+        q_mean[...] = mean
+        high, low = split(mean)
+        factors[...] = jnp.concatenate([high, low, high], axis=0)
+
+    high, low = split(basis[...])
+    approx = dot(jnp.concatenate([high, high, low], axis=0), factors[...], COLUMNS)
+    error_next[...] = (merged[...] - approx).astype(BF16)
+
+
+def finish(merged, basis, terms, scale, block):
+    wide, cols = merged.shape
+    rank = basis.shape[0]
+    return pl.pallas_call(
+        functools.partial(finish_body, scale),
+        grid=(wide // block,),
+        in_specs=[
+            pl.BlockSpec((block, cols), lambda i: (i, 0)),
+            pl.BlockSpec((rank, block), lambda i: (0, i)),
+            pl.BlockSpec(terms.shape, lambda i: (0, 0, 0)),
+        ],
+        out_specs=[
+            pl.BlockSpec((block, cols), lambda i: (i, 0)),
+            pl.BlockSpec((rank, cols), lambda i: (0, 0)),
+        ],
+        out_shape=[
+            jax.ShapeDtypeStruct((wide, cols), BF16),
+            jax.ShapeDtypeStruct((rank, cols), F32),
+        ],
+        scratch_shapes=[pltpu.VMEM((3 * rank, cols), BF16)],
+        compiler_params=pltpu.CompilerParams(vmem_limit_bytes=24 * 2**20),
+        cost_estimate=pl.CostEstimate(
+            flops=6 * rank * wide * cols, bytes_accessed=6 * wide * cols, transcendentals=0
+        ),
+        name="finish",
+    )(merged, basis, terms)
 
 
 def on_device(normed, key_grad, error_in, q_init):
@@ -62,14 +162,11 @@
     inverse = lax.linalg.triangular_solve(lower, jnp.eye(rank, dtype=F32), left_side=True, lower=True)
     p_basis = jnp.dot(inverse, p_sum, precision=HIGH)
 
-    merged = lax.dot_general(gathered, grads, (((0,), (0,)), ((), ())), preferred_element_type=F32)
-    merged = merged + errors.astype(F32)
-    q_local = jnp.dot(p_basis, merged, precision=HIGH)
+    merged, q_local = merge(gathered, grads, errors, p_basis, 1024)
     q_local = q_local + lax.ppermute(q_local, "c", [(0, 1), (1, 0)])
-    q_mean = jnp.sum(spread(q_local.astype(BF16), PLANE).astype(F32), axis=0) / replicas
-    approx = lax.dot_general(p_basis, q_mean, (((0,), (0,)), ((), ())), precision=HIGH)
-    error_next = (merged - approx).astype(BF16)[None]
-    return (error_next, p_basis.T, q_mean.T)
+    q_local = jnp.sum(spread(q_local, "x"), axis=0)
+    error_next, q_mean = finish(merged, p_basis, spread(q_local, "y"), 1.0 / replicas, 2048)
+    return (error_next[None], p_basis.T, q_mean.T)
 
 
 def solution(mesh):

time: 160 us -> 157 us (0.981)
  Pallas kernels: 0 us -> 7.42 us
  matrix products: 13.2 us -> 6.24 us
  blocking collectives: 115 us -> 111 us
  waiting for transfers between devices: 3.32 us -> 1.52 us
  starting transfers between devices: 2.94 us -> 4.58 us
    dot_general x3 -> x0, matrix products: 10.3 us -> none  [the longest x1 4.68 us: on_device(): lax.dot_general(gathered, grads, (((0,), (0,)), ((), ())), preferred_elem...]
    pallas_call x0 -> x2, Pallas kernels: none -> 7.42 us  [the longest x1 5.86 us: merge(): pl.pallas_call(merge_body, grid=(wide // block,), in_specs=[pl.BlockSpec(...]
    all_to_all x5 -> x6, blocking collectives: 115 us -> 111 us  [swap(): return lax.all_to_all(value, axes, 0, 0, tiled=True)]
    all_gather x1, waiting for transfers between devices: 1.82 us -> 0.02 us  [on_device(): gathered = lax.all_gather(inputs, 'z', axis=0, tiled=True)]
    ppermute x1, starting transfers between devices: 2.9 us -> 4.54 us  [on_device(): q_local = q_local + lax.ppermute(q_local, 'c', [(0, 1), (1, 0)])]
  transfers between devices with their start and end apart: 2 -> 2, of which waited for: 2 -> 1; matrix products, arithmetic and copies ran while one was open for 7% -> 9% of each run, Pallas kernels for 0% -> 0%
where the time goes in v2:
time: 157 us; the launch traced here: 155 us
  blocking collectives  111 us (71%)
  between operations  14.2 us (9%)
  other arithmetic  7.64 us (5%)
  Pallas kernels  7.42 us (5%)
  matrix products  6.24 us (4%)
  starting transfers between devices  4.58 us (3%)
  local copies, waits for them, and re-layouts  2.2 us (1%)
    all_to_all x6, blocking collectives, swap(): return lax.all_to_all(value, axes, 0, 0, tiled=True)  111 us
    pallas_call x1, Pallas kernels, merge(): pl.pallas_call(merge_body, grid=(wide // block,), in_specs=[pl.BlockSpec(...  5.86 us
    ppermute x1, starting transfers between devices, on_device(): q_local = q_local + lax.ppermute(q_local, 'c', [(0, 1), (1, 0)])  4.54 us
    another operation x3, other arithmetic, on_device(): lower = jnp.linalg.cholesky(gram)  3.6 us
  transfers between devices with their start and end apart: 2, of which 1 were waited for; matrix products, arithmetic and copies ran while one was open for 9% of the time, Pallas kernels for 0%

profile of v2, /device:TPU:1, one launch (start us, length us, event | category | flops | bytes accessed | tf_op | source)
XLA Modules:
  0.0 155.1 jit_solution(9944129601612422868)
XLA Ops:
  7.2 0.0 all-gather.3.cloned.1.call-start
  7.2 0.7 all-gather.3.cloned.1.call-update
  7.9 0.7 reduce-precision_convert_fusion.1
  8.6 1.1 fusion.19
  9.8 0.1 reshape.32
  9.9 24.8 %all_to_all.30 = f32[8,32,96]{2,1,0:T(8,128)S(1)} all-to-all(f32[8,32,96]{2,1,0:T(8,128)S(1)} %bitcast.55), channel_id=1, replica_groups=mesh['x'=8,'y'=8,'c'=2,'z'=8] {'z'}, dimensions={0} | all-to-all | bytes 196608 | tf_op jit(solution)/shard_map/all_to_all | solution.py:31
  34.8 1.5 fusion
  36.3 1.7 %convolution_add_fusion = f32[64,4096]{1,0:T(8,128)S(1)} fusion(f32[64,4096]{1,0:T(8,128)S(1)} %fusion, bf16[32,128]{1,0:T(8,128)(2,1)S(1)} %get-tuple-element.14, bf16[32,128]{1,0:T(8,128)(2,1)S(1)} %get-tuple-element.13, bf16[1,4096,128]{2,1,0:T(8,128)(2,1)} %param.6), kind=kOutput, calls=%fused_computation | convolution fusion | flops 67403776 | bytes 3162112 | tf_op jit(solution)/shard_map/dot_general | solution.py:147
  38.0 0.1 fusion.9
  38.1 0.1 copy.18
  38.2 25.5 %all_to_all.31 = bf16[64,16,128]{2,1,0:T(8,128)(2,1)S(1)} all-to-all(bf16[64,16,128]{2,1,0:T(8,128)(2,1)S(1)} %bitcast.54), channel_id=1, replica_groups=mesh['x'=8,'y'=8,'c'=2,'z'=8] {'x','y'}, dimensions={0} | all-to-all | bytes 524288 | tf_op jit(solution)/shard_map/all_to_all | solution.py:31
  63.7 0.1 convert_reduce_fusion
  63.8 15.4 %all_to_all.32 = f32[16,16,128]{2,1,0:T(8,128)S(1)} all-to-all(f32[16,16,128]{2,1,0:T(8,128)S(1)} %broadcast_in_dim.12), channel_id=1, replica_groups=mesh['x'=8,'y'=8,'c'=2,'z'=8] {'c','z'}, dimensions={0} | all-to-all | bytes 262144 | tf_op jit(solution)/shard_map/all_to_all | solution.py:31
  79.2 20.9 %all_to_all.33 = f32[64,16,128]{2,1,0:T(8,128)S(1)} all-to-all(f32[64,16,128]{2,1,0:T(8,128)S(1)} %broadcast_in_dim.13), channel_id=1, replica_groups=mesh['x'=8,'y'=8,'c'=2,'z'=8] {'x','y'}, dimensions={0} | all-to-all | bytes 1048576 | tf_op jit(solution)/shard_map/all_to_all | solution.py:31
  100.2 0.2 copy.19
  100.3 0.8 fusion.4
  101.2 0.1 copy.20
  101.2 2.9 %cholesky.17 = f32[32,32]{1,0:T(8,128)S(1)} custom-call(f32[32,32]{1,0:T(8,128)S(1)} %fusion.18), custom_call_target="Cholesky" | custom-call | tf_op jit(solution)/shard_map/jit(cholesky)/cholesky | solution.py:161
  104.2 0.6 compare_reduce_fusion
  104.8 0.7 fusion.10
  105.5 2.5 %custom-call.6 = f32[1,32,32]{1,2,0:T(8,128)S(1)} custom-call(f32[1,32,32]{2,1,0:T(8,128)S(1)} %fusion.10), custom_call_target="InvertDiagBlocksLowerTriangular" | custom-call | tf_op jit(solution)/shard_map/triangular_solve | solution.py:162
  108.0 0.2 fusion.16
  108.2 0.9 fusion.2.basis
  109.0 0.0 copy-start
  109.1 0.0 all-gather.3.cloned.1.call-done
  109.1 5.9 %merge.1 = (f32[4096,128]{1,0:T(8,128)}, f32[32,128]{1,0:T(8,128)S(1)}) custom-call(bf16[768,4096]{1,0:T(8,128)(2,1)} %bitcast.49, bf16[768,128]{1,0:T(8,128)(2,1)S(1)} %bitcast.48, bf16[4096,128]{1,0:T(8,128)(2,1)S(1)} %bitcast.47, f32[32,4096]{1,0:T(8,128)S(1)} %fusion.2.basis), custom_call_target="tpu_custom_call" | custom-call | flops 805306368 | bytes 6291456 | tf_op jit(solution)/shard_map/merge/pallas_call | solution.py:65
  115.0 4.5 %collective-permute-start = (f32[32,128]{1,0:T(8,128)S(1)}, f32[32,128]{1,0:T(8,128)S(1)}, u32[]{:S(2)}, u32[]{:S(2)}) collective-permute-start(f32[32,128]{1,0:T(8,128)S(1)} %get-tuple-element.8), channel_id=1, source_target_pairs={{0,8},{8,0},{1,9},{9,1},{2,10},{10,2},{3,11},{11,3},{4,12},{12,4},... | collective-permute-start | bytes 49160 | tf_op jit(solution)/shard_map/ppermute | solution.py:166
  119.5 0.8 collective-permute-done
  120.4 12.0 %all_to_all.34 = f32[8,32,128]{2,1,0:T(8,128)S(1)} all-to-all(f32[8,32,128]{2,1,0:T(8,128)S(1)} %broadcast_in_dim.14), channel_id=1, replica_groups=mesh['x'=8,'y'=8,'c'=2,'z'=8] {'x'}, dimensions={0} | all-to-all | bytes 262144 | tf_op jit(solution)/shard_map/all_to_all | solution.py:31
  132.4 12.7 %all_to_all.35.terms = f32[8,32,128]{2,1,0:T(8,128)S(1)} all-to-all(f32[8,32,128]{2,1,0:T(8,128)S(1)} %broadcast_in_dim.15), channel_id=1, replica_groups=mesh['x'=8,'y'=8,'c'=2,'z'=8] {'y'}, dimensions={0} | all-to-all | bytes 262144 | tf_op jit(solution)/shard_map/all_to_all | solution.py:31
  145.1 1.6 %copy-done.2 = f32[4096,128]{1,0:T(8,128)S(1)} copy-done((f32[4096,128]{1,0:T(8,128)S(1)}, f32[4096,128]{1,0:T(8,128)}, u32[]{:S(2)}) %copy-start.2) | copy-done | bytes 2097176
  146.7 1.6 %finish.1 = (bf16[4096,128]{1,0:T(8,128)(2,1)}, f32[32,128]{1,0:T(8,128)}) custom-call(f32[4096,128]{1,0:T(8,128)S(1)} %copy-done.2, f32[32,4096]{1,0:T(8,128)S(1)} %fusion.2.basis, f32[8,32,128]{2,1,0:T(8,128)S(1)} %all_to_all.35.terms), custom_call_target="tpu_custom_call" | custom-call | flops 100663296 | bytes 3145728 | tf_op jit(solution)/shard_map/finish/pallas_call | solution.py:107
  (20 shorter events, 0.3 us)
Async XLA Ops:
  7.2 101.9 %all-gather.3.cloned.1.call-start = ((), (), s32[]{:S(2)}) async-start(), calls=%async_computation.6 | async-start | bytes 7077888 | tf_op jit(solution)/shard_map/all_gather | solution.py:139
  34.7 74.3 %copy-start.1 = (bf16[1,4096,128]{2,1,0:T(8,128)(2,1)S(1)}, bf16[1,4096,128]{2,1,0:T(8,128)(2,1)}, u32[]{:S(2)}) copy-start(bf16[1,4096,128]{2,1,0:T(8,128)(2,1)} %param.6) | copy-start | bytes 3145732
  34.8 74.3 %copy-start.3 = (bf16[1,768,128]{2,1,0:T(8,128)(2,1)S(1)}, bf16[1,768,128]{2,1,0:T(8,128)(2,1)}, u32[]{:S(2)}) copy-start(bf16[1,768,128]{2,1,0:T(8,128)(2,1)} %param.5) | copy-start | bytes 589828
  109.0 39.2 %copy-start = (f32[32,4096]{1,0:T(8,128)}, f32[32,4096]{1,0:T(8,128)S(1)}, u32[]{:S(2)}) copy-start(f32[32,4096]{1,0:T(8,128)S(1)} %fusion.2.basis) | copy-start | bytes 1572868
  115.0 5.4 %collective-permute-start = (f32[32,128]{1,0:T(8,128)S(1)}, f32[32,128]{1,0:T(8,128)S(1)}, u32[]{:S(2)}, u32[]{:S(2)}) collective-permute-start(f32[32,128]{1,0:T(8,128)S(1)} %get-tuple-element.8), channel_id=1, source_target_pairs={{0,8},{8,0},{1,9},{9,1},{2,10},{10,2},{3,11},{11,3},{4,12},{12,4},... | collective-permute-start | bytes 49160 | tf_op jit(solution)/shard_map/ppermute | solution.py:166
  145.1 1.6 %copy-start.2 = (f32[4096,128]{1,0:T(8,128)S(1)}, f32[4096,128]{1,0:T(8,128)}, u32[]{:S(2)}) copy-start(f32[4096,128]{1,0:T(8,128)} %get-tuple-element.7.merged) | copy-start | bytes 6291460
Sparse Core Ops, SparseCore 0:
  10.7 96.9 all-gather.2

commit v3 on v2

--- a/solution.py
+++ b/solution.py
@@ -44,54 +44,51 @@
     return head, (value - head.astype(F32)).astype(BF16)
 
 
-def merge_body(inputs, grads, errors, basis, merged, q_out, turned):
+def merge_body(count, *refs):
+    parts, (grads, errors, merged, turned) = refs[:count], refs[count:]
+
     @pl.when(pl.program_id(0) == 0)
     def _():
-        q_out[...] = jnp.zeros_like(q_out)
         turned[...] = grads[...].T
 
-    block = dot(turned[...], inputs[...]).T + errors[...].astype(F32)
-    merged[...] = block
-    high, low = split(block)
-    b_high, b_low = split(basis[...])
-    rank = b_high.shape[0]
-    q = dot(jnp.concatenate([b_high, b_low], axis=0), high)
-    q_out[...] += q[:rank] + q[rank:] + dot(b_high, low)
+    inputs = jnp.concatenate([part[...] for part in parts], axis=0)
+    merged[...] = dot(turned[...], inputs).T + errors[...].astype(F32)
 
 
-def merge(inputs, grads, errors, basis, block):
-    tokens, wide = inputs.shape
-    cols, rank = grads.shape[1], basis.shape[0]
+def merge(parts, grads, errors, block):
+    count = len(parts)
+    rows, wide = parts[0].shape
+    tokens, cols = grads.shape
     return pl.pallas_call(
-        merge_body,
+        functools.partial(merge_body, count),
         grid=(wide // block,),
-        in_specs=[
-            pl.BlockSpec((tokens, block), lambda i: (0, i)),
+        in_specs=[pl.BlockSpec((rows, block), lambda i: (0, i)) for _ in parts]
+        + [
             pl.BlockSpec((tokens, cols), lambda i: (0, 0)),
             pl.BlockSpec((block, cols), lambda i: (i, 0)),
-            pl.BlockSpec((rank, block), lambda i: (0, i)),
         ],
-        out_specs=[
-            pl.BlockSpec((block, cols), lambda i: (i, 0)),
-            pl.BlockSpec((rank, cols), lambda i: (0, 0)),
-        ],
-        out_shape=[
-            jax.ShapeDtypeStruct((wide, cols), F32),
-            jax.ShapeDtypeStruct((rank, cols), F32),
-        ],
+        out_specs=pl.BlockSpec((block, cols), lambda i: (i, 0)),
+        out_shape=jax.ShapeDtypeStruct((wide, cols), F32),
         scratch_shapes=[pltpu.VMEM((cols, tokens), BF16)],
-        compiler_params=pltpu.CompilerParams(vmem_limit_bytes=52 * 2**20),
+        compiler_params=pltpu.CompilerParams(vmem_limit_bytes=24 * 2**20),
         cost_estimate=pl.CostEstimate(
             flops=2 * tokens * wide * cols, bytes_accessed=2 * tokens * wide, transcendentals=0
         ),
         name="merge",
-    )(inputs, grads, errors, basis)
+    )(*parts, grads, errors)
+
+
+def in_order(grads, axis, rows, order):
+    size = lax.axis_size(axis)
+    twice = jnp.concatenate([grads, grads], axis=0)
+    turned = lax.dynamic_slice_in_dim(twice, lax.axis_index(axis) * rows, size * rows, axis=0)
+    return jnp.concatenate([turned[(o % size) * rows : (o % size + 1) * rows] for o in order], axis=0)
 
 
 def finish_body(scale, merged, basis, terms, error_next, q_mean, factors):
     @pl.when(pl.program_id(0) == 0)
     def _():
-        mean = jnp.sum(terms[...], axis=0) * scale
+        mean = jnp.sum(terms[...].astype(F32), axis=0) * scale
         q_mean[...] = mean
         high, low = split(mean)
         factors[...] = jnp.concatenate([high, low, high], axis=0)
@@ -136,7 +133,16 @@
     replicas = plane * lax.axis_size("c")
     tokens, wide = inputs.shape
     rank = q_init.shape[1]
-    gathered = lax.all_gather(inputs, "z", axis=0, tiled=True)
+    ahead = [(i, (i + 1) % tp) for i in range(tp)]
+    back = [(i, (i - 1) % tp) for i in range(tp)]
+    up, down, order = [inputs], [inputs], [0]
+    for step in range(1, tp // 2 + 1):
+        up.append(lax.ppermute(up[-1], "z", ahead))
+        order.append(-step)
+        if 2 * step < tp:
+            down.append(lax.ppermute(down[-1], "z", back))
+            order.append(step)
+    parts = [inputs] + [p for pair in zip(up[1:], down[1:]) for p in pair] + up[len(down) :]
 
     q_terms = two_terms(q_init.T)
     by_head = fold(lax.dot_general(q_terms, grads, (((1,), (1,)), ((), ())), preferred_element_type=F32))
@@ -151,21 +157,28 @@
     halves = plane // columns
     depth = rank // halves
     pieces = jnp.transpose(p_local.reshape(halves, depth, columns, lanes), (0, 2, 1, 3))
-    pieces = pieces.reshape(plane, depth, lanes).astype(BF16)
-    piece = jnp.sum(swap(pieces, PLANE).astype(F32), axis=0)
+    pieces = pieces.reshape(plane, depth, lanes)
+    piece = jnp.sum(swap(pieces, PLANE), axis=0)
     piece = jnp.sum(spread(piece, ("c", "z")), axis=0)
     p_sum = spread(piece, PLANE).reshape(halves, columns, depth, lanes)
     p_sum = jnp.transpose(p_sum, (0, 2, 1, 3)).reshape(rank, wide)
+
+    p_terms = two_terms(p_sum)
+    met = fold(dot(p_terms, inputs, ROWS))
+    met = spread(met, "z")
+    q_raw = fold(dot(p_terms, errors))
+    met = jnp.transpose(met, (1, 0, 2)).reshape(rank, tp * tokens)
+    q_raw = q_raw + fold(dot(two_terms(met), grads))
 
     gram = lax.dot_general(p_sum, p_sum, (((1,), (1,)), ((), ())), precision=HIGH)
     lower = jnp.linalg.cholesky(gram)
     inverse = lax.linalg.triangular_solve(lower, jnp.eye(rank, dtype=F32), left_side=True, lower=True)
     p_basis = jnp.dot(inverse, p_sum, precision=HIGH)
+    q_local = jnp.dot(inverse, q_raw, precision=HIGH)
 
-    merged, q_local = merge(gathered, grads, errors, p_basis, 1024)
-    q_local = q_local + lax.ppermute(q_local, "c", [(0, 1), (1, 0)])
-    q_local = jnp.sum(spread(q_local, "x"), axis=0)
-    error_next, q_mean = finish(merged, p_basis, spread(q_local, "y"), 1.0 / replicas, 2048)
+    merged = merge(parts, in_order(grads, "z", tokens, order), errors, 1024)
+    q_local = jnp.sum(spread(q_local, ("y", "c")), axis=0)
+    error_next, q_mean = finish(merged, p_basis, spread(q_local, "x"), 1.0 / replicas, 2048)
     return (error_next[None], p_basis.T, q_mean.T)
 
 

time: 157 us -> 178 us (1.13)
  blocking collectives: 111 us -> 15.6 us
  starting transfers between devices: 4.58 us -> 80.9 us
  waiting for transfers between devices: 1.52 us -> 49.2 us
  between operations: 14.2 us -> 1.04 us
  local copies, waits for them, and re-layouts: 2.2 us -> 9.77 us
    all_to_all x6 -> x1, blocking collectives: 111 us -> 15.6 us  [swap(): return lax.all_to_all(value, axes, 0, 0, tiled=True)]
    all_to_all x0 -> x6, starting transfers between devices: none -> 61.5 us  [swap(): return lax.all_to_all(value, axes, 0, 0, tiled=True)]
    all_to_all x0 -> x6, waiting for transfers between devices: none -> 34.1 us  [swap(): return lax.all_to_all(value, axes, 0, 0, tiled=True)]
    ppermute x1 -> x7, starting transfers between devices: 4.54 us -> 19.4 us  [the longest x4 12.7 us: on_device(): up.append(lax.ppermute(up[-1], 'z', ahead))]
    ppermute x1 -> x7, waiting for transfers between devices: 0.82 us -> 15.1 us  [the longest x3 15 us: on_device(): down.append(lax.ppermute(down[-1], 'z', back))]
    broadcast_in_dim x4 -> x5, local copies, waits for them, and re-layouts: 0.07 us -> 2.93 us  [spread(): jnp.broadcast_to(value[None], (lax.axis_size(axes),) + value.shape)]
    unnamed x9 -> x27, local copies, waits for them, and re-layouts: 1.65 us -> 3.49 us
  transfers between devices with their start and end apart: 2 -> 13, of which waited for: 1 -> 6; matrix products, arithmetic and copies ran while one was open for 9% -> 10% of each run, Pallas kernels for 0% -> 3%
where the time goes in v3:
time: 178 us; the launch traced here: 177 us
  starting transfers between devices  80.9 us (45%)
  waiting for transfers between devices  49.2 us (28%)
  blocking collectives  15.6 us (9%)
  local copies, waits for them, and re-layouts  9.77 us (5%)
  other arithmetic  8.78 us (5%)
  Pallas kernels  6.01 us (3%)
  matrix products  5.58 us (3%)
    all_to_all x6, starting transfers between devices, swap(): return lax.all_to_all(value, axes, 0, 0, tiled=True)  61.5 us
    all_to_all x6, waiting for transfers between devices, swap(): return lax.all_to_all(value, axes, 0, 0, tiled=True)  34.1 us
    all_to_all x1, blocking collectives, swap(): return lax.all_to_all(value, axes, 0, 0, tiled=True)  15.6 us
    ppermute x3, waiting for transfers between devices, on_device(): down.append(lax.ppermute(down[-1], 'z', back))  15 us
    ppermute x4, starting transfers between devices, on_device(): up.append(lax.ppermute(up[-1], 'z', ahead))  12.7 us
    ppermute x3, starting transfers between devices, on_device(): down.append(lax.ppermute(down[-1], 'z', back))  6.76 us
    pallas_call x1, Pallas kernels, merge(): pl.pallas_call(functools.partial(merge_body, count), grid=(wide // block,...  4.45 us
    another operation x3, other arithmetic, on_device(): lower = jnp.linalg.cholesky(gram)  3.6 us
  transfers between devices with their start and end apart: 13, of which 6 were waited for; matrix products, arithmetic and copies ran while one was open for 10% of the time, Pallas kernels for 3%

profile of v3, /device:TPU:1, one launch (start us, length us, event | category | flops | bytes accessed | tf_op | source)
XLA Modules:
  0.0 176.9 jit_solution(14745376455342114268)
XLA Ops:
  0.7 0.9 reduce-precision_convert_fusion.3
  1.5 1.1 fusion.31
  3.4 17.2 %all-to-all-start = ((f32[8,32,96]{2,1,0:T(8,128)}), f32[8,32,96]{2,1,0:T(8,128)S(1)}, u32[]{:S(2)}, u32[]{:S(2)}) async-start(f32[8,32,96]{2,1,0:T(8,128)} %bitcast.54), calls=%async_computation | async-start | bytes 262144 | tf_op jit(solution)/shard_map/all_to_all | solution.py:31
  20.7 3.4 %collective-permute-start = (bf16[96,4096]{1,0:T(8,128)(2,1)}, bf16[96,4096]{1,0:T(8,128)(2,1)S(1)}, u32[]{:S(2)}, u32[]{:S(2)}) collective-permute-start(bf16[96,4096]{1,0:T(8,128)(2,1)} %bitcast.56), channel_id=1, source_target_pairs={{0,1},{1,2},{2,3},{3,4},{4,5},{5,6},{6,7},{7,0},{8,9},{9,10},{10,1... | collective-permute-start | bytes 2359304 | tf_op jit(solution)/shard_map/ppermute | solution.py:140
  24.0 4.4 %all-to-all-done = f32[8,32,96]{2,1,0:T(8,128)S(1)} async-done(((f32[8,32,96]{2,1,0:T(8,128)}), f32[8,32,96]{2,1,0:T(8,128)S(1)}, u32[]{:S(2)}, u32[]{:S(2)}) %all-to-all-start) | async-done | bytes 98336 | tf_op jit(solution)/shard_map/all_to_all | solution.py:31
  29.5 1.1 copy.19
  30.6 13.3 %all-to-all-start.1 = ((f32[64,16,128]{2,1,0:T(8,128)}), f32[64,16,128]{2,1,0:T(8,128)S(1)}, u32[]{:S(2)}, u32[]{:S(2)}) async-start(f32[64,16,128]{2,1,0:T(8,128)} %bitcast.63), calls=%async_computation.1 | async-start | bytes 1048576 | tf_op jit(solution)/shard_map/all_to_all | solution.py:31
  43.9 1.9 %collective-permute-start.1 = (bf16[96,4096]{1,0:T(8,128)(2,1)S(1)}, bf16[96,4096]{1,0:T(8,128)(2,1)}, u32[]{:S(2)}, u32[]{:S(2)}) collective-permute-start(bf16[96,4096]{1,0:T(8,128)(2,1)S(1)} %bitcast.57), channel_id=1, source_target_pairs={{0,7},{1,0},{2,1},{3,2},{4,3},{5,4},{6,5},{7,6},{8,15},{9,8},{10,9... | collective-permute-start | bytes 2359304 | tf_op jit(solution)/shard_map/ppermute | solution.py:143
  45.9 3.4 %collective-permute-start.2 = (bf16[96,4096]{1,0:T(8,128)(2,1)S(1)}, bf16[96,4096]{1,0:T(8,128)(2,1)}, u32[]{:S(2)}, u32[]{:S(2)}) collective-permute-start(bf16[96,4096]{1,0:T(8,128)(2,1)S(1)} %collective-permute-done.refs_1_), channel_id=1, source_target_pairs={{0,1},{1,2},{2,3},{3,4},{4,5},{5,6},{6,7},{7,0},{8,9},{9,10},{10,1... | collective-permute-start | bytes 2359304 | tf_op jit(solution)/shard_map/ppermute | solution.py:140
  49.3 9.4 %all-to-all-done.1 = f32[64,16,128]{2,1,0:T(8,128)S(1)} async-done(((f32[64,16,128]{2,1,0:T(8,128)}), f32[64,16,128]{2,1,0:T(8,128)S(1)}, u32[]{:S(2)}, u32[]{:S(2)}) %all-to-all-start.1) | async-done | bytes 524320 | tf_op jit(solution)/shard_map/all_to_all | solution.py:31
  58.7 15.6 %all_to_all.35 = f32[16,16,128]{2,1,0:T(8,128)S(1)} all-to-all(f32[16,16,128]{2,1,0:T(8,128)S(1)} %broadcast_in_dim.14), channel_id=1, replica_groups=mesh['x'=8,'y'=8,'c'=2,'z'=8] {'c','z'}, dimensions={0} | all-to-all | bytes 262144 | tf_op jit(solution)/shard_map/all_to_all | solution.py:31
  75.2 9.0 %all-to-all-start.3 = ((f32[64,16,128]{2,1,0:T(8,128)}), f32[64,16,128]{2,1,0:T(8,128)}, u32[]{:S(2)}, u32[]{:S(2)}) async-start(f32[64,16,128]{2,1,0:T(8,128)} %broadcast_in_dim.15), calls=%async_computation.3 | async-start | bytes 1048576 | tf_op jit(solution)/shard_map/all_to_all | solution.py:31
  85.0 1.9 %collective-permute-start.3 = (bf16[96,4096]{1,0:T(8,128)(2,1)}, bf16[96,4096]{1,0:T(8,128)(2,1)}, u32[]{:S(2)}, u32[]{:S(2)}) collective-permute-start(bf16[96,4096]{1,0:T(8,128)(2,1)} %collective-permute-done.1.refs_2_), channel_id=1, source_target_pairs={{0,7},{1,0},{2,1},{3,2},{4,3},{5,4},{6,5},{7,6},{8,15},{9,8},{10,9... | collective-permute-start | bytes 2359304 | tf_op jit(solution)/shard_map/ppermute | solution.py:143
  86.9 3.4 %collective-permute-start.4 = (bf16[96,4096]{1,0:T(8,128)(2,1)}, bf16[96,4096]{1,0:T(8,128)(2,1)}, u32[]{:S(2)}, u32[]{:S(2)}) collective-permute-start(bf16[96,4096]{1,0:T(8,128)(2,1)} %collective-permute-done.2.refs_3_), channel_id=1, source_target_pairs={{0,1},{1,2},{2,3},{3,4},{4,5},{5,6},{6,7},{7,0},{8,9},{9,10},{10,1... | collective-permute-start | bytes 2359304 | tf_op jit(solution)/shard_map/ppermute | solution.py:140
  90.4 15.0 %collective-permute-done.3.refs_4_ = bf16[96,4096]{1,0:T(8,128)(2,1)} collective-permute-done((bf16[96,4096]{1,0:T(8,128)(2,1)}, bf16[96,4096]{1,0:T(8,128)(2,1)}, u32[]{:S(2)}, u32[]{:S(2)}) %collective-permute-start.3) | collective-permute-done | bytes 786464 | tf_op jit(solution)/shard_map/ppermute | solution.py:143
  105.4 2.9 %collective-permute-start.5 = (bf16[96,4096]{1,0:T(8,128)(2,1)}, bf16[96,4096]{1,0:T(8,128)(2,1)}, u32[]{:S(2)}, u32[]{:S(2)}) collective-permute-start(bf16[96,4096]{1,0:T(8,128)(2,1)} %collective-permute-done.3.refs_4_), channel_id=1, source_target_pairs={{0,7},{1,0},{2,1},{3,2},{4,3},{5,4},{6,5},{7,6},{8,15},{9,8},{10,9... | collective-permute-start | bytes 2359304 | tf_op jit(solution)/shard_map/ppermute | solution.py:143
  108.3 2.6 %collective-permute-start.6 = (bf16[96,4096]{1,0:T(8,128)(2,1)}, bf16[96,4096]{1,0:T(8,128)(2,1)}, u32[]{:S(2)}, u32[]{:S(2)}) collective-permute-start(bf16[96,4096]{1,0:T(8,128)(2,1)} %collective-permute-done.4.refs_5_), channel_id=1, source_target_pairs={{0,1},{1,2},{2,3},{3,4},{4,5},{5,6},{6,7},{7,0},{8,9},{9,10},{10,1... | collective-permute-start | bytes 2359304 | tf_op jit(solution)/shard_map/ppermute | solution.py:140
  111.0 1.2 copy.20
  114.2 2.9 %cholesky.17 = f32[32,32]{1,0:T(8,128)S(1)} custom-call(f32[32,32]{1,0:T(8,128)S(1)} %fusion.30), custom_call_target="Cholesky" | custom-call | tf_op jit(solution)/shard_map/jit(cholesky)/cholesky | solution.py:174
  118.4 2.4 %custom-call.6 = f32[1,32,32]{1,2,0:T(8,128)S(1)} custom-call(f32[1,32,32]{2,1,0:T(8,128)S(1)} %fusion.16), custom_call_target="InvertDiagBlocksLowerTriangular" | custom-call | tf_op jit(solution)/shard_map/triangular_solve | solution.py:175
  121.6 5.1 %all-to-all-start.4 = ((f32[8,32,96]{2,1,0:T(8,128)}), f32[8,32,96]{2,1,0:T(8,128)S(1)}, u32[]{:S(2)}, u32[]{:S(2)}) async-start(f32[8,32,96]{2,1,0:T(8,128)} %broadcast_in_dim.16), calls=%async_computation.4 | async-start | bytes 262144 | tf_op jit(solution)/shard_map/all_to_all | solution.py:31
  126.9 7.4 %all-to-all-done.4 = f32[8,32,96]{2,1,0:T(8,128)S(1)} async-done(((f32[8,32,96]{2,1,0:T(8,128)}), f32[8,32,96]{2,1,0:T(8,128)S(1)}, u32[]{:S(2)}, u32[]{:S(2)}) %all-to-all-start.4) | async-done | bytes 98336 | tf_op jit(solution)/shard_map/all_to_all | solution.py:31
  135.6 10.2 %all-to-all-start.5 = ((f32[16,32,128]{2,1,0:T(8,128)}), f32[16,32,128]{2,1,0:T(8,128)S(1)}, u32[]{:S(2)}, u32[]{:S(2)}) async-start(f32[16,32,128]{2,1,0:T(8,128)} %broadcast_in_dim.17), calls=%async_computation.5 | async-start | bytes 524288 | tf_op jit(solution)/shard_map/all_to_all | solution.py:31
  145.9 11.7 %all-to-all-done.5 = f32[16,32,128]{2,1,0:T(8,128)S(1)} async-done(((f32[16,32,128]{2,1,0:T(8,128)}), f32[16,32,128]{2,1,0:T(8,128)S(1)}, u32[]{:S(2)}, u32[]{:S(2)}) %all-to-all-start.5) | async-done | bytes 262176 | tf_op jit(solution)/shard_map/all_to_all | solution.py:31
  158.2 6.5 %all-to-all-start.6 = ((f32[8,32,128]{2,1,0:T(8,128)}), f32[8,32,128]{2,1,0:T(8,128)S(1)}, u32[]{:S(2)}, u32[]{:S(2)}) async-start(f32[8,32,128]{2,1,0:T(8,128)} %broadcast_in_dim.18), calls=%async_computation.6 | async-start | bytes 262144 | tf_op jit(solution)/shard_map/all_to_all | solution.py:31
  164.7 1.7 fusion.1.basis
  166.4 1.1 copy-done.2
  167.5 1.1 copy-done.5
  168.6 4.4 %merge.1.merged = f32[4096,128]{1,0:T(8,128)S(1)} custom-call(bf16[96,4096]{1,0:T(8,128)(2,1)S(1)} %bitcast.58, bf16[96,4096]{1,0:T(8,128)(2,1)S(1)} %copy-done.5, bf16[96,4096]{1,0:T(8,128)(2,1)} %collective-permute-done.1.refs_2_, bf16[96,4096]{1,0:T(8,128)(2,1)} %collective-permute-done.2.refs_3_, bf16[96,4096]{1,0:T(8,128)(2,1)} %collective-permute-done.3.refs_4_, ...), custom_call_target="tpu_custom_call" | custom-call | flops 805306368 | bytes 6291456 | tf_op jit(solution)/shard_map/merge/pallas_call | solution.py:62
  173.1 1.2 all-to-all-done.6.terms
  174.3 1.0 copy-done.3
  175.3 1.6 finish.1
  (65 shorter events, 9.6 us)
Async XLA Ops:
  0.6 27.9 %copy-start.1 = (bf16[1,96,4096]{2,1,0:T(8,128)(2,1)S(1)}, bf16[1,96,4096]{2,1,0:T(8,128)(2,1)}, u32[]{:S(2)}) copy-start(bf16[1,96,4096]{2,1,0:T(8,128)(2,1)} %param.4) | copy-start | bytes 2359300
  0.6 28.2 %copy-start = (bf16[1,4096,128]{2,1,0:T(8,128)(2,1)S(1)}, bf16[1,4096,128]{2,1,0:T(8,128)(2,1)}, u32[]{:S(2)}) copy-start(bf16[1,4096,128]{2,1,0:T(8,128)(2,1)} %param.6) | copy-start | bytes 3145732
  3.4 25.0 %all-to-all-start = ((f32[8,32,96]{2,1,0:T(8,128)}), f32[8,32,96]{2,1,0:T(8,128)S(1)}, u32[]{:S(2)}, u32[]{:S(2)}) async-start(f32[8,32,96]{2,1,0:T(8,128)} %bitcast.54), calls=%async_computation | async-start | bytes 262144 | tf_op jit(solution)/shard_map/all_to_all | solution.py:31
  20.7 25.2 %collective-permute-start = (bf16[96,4096]{1,0:T(8,128)(2,1)}, bf16[96,4096]{1,0:T(8,128)(2,1)S(1)}, u32[]{:S(2)}, u32[]{:S(2)}) collective-permute-start(bf16[96,4096]{1,0:T(8,128)(2,1)} %bitcast.56), channel_id=1, source_target_pairs={{0,1},{1,2},{2,3},{3,4},{4,5},{5,6},{6,7},{7,0},{8,9},{9,10},{10,1... | collective-permute-start | bytes 2359304 | tf_op jit(solution)/shard_map/ppermute | solution.py:140
  30.6 53.7 %copy-start.6 = (bf16[1,768,128]{2,1,0:T(8,128)(2,1)S(1)}, bf16[1,768,128]{2,1,0:T(8,128)(2,1)}, u32[]{:S(2)}) copy-start(bf16[1,768,128]{2,1,0:T(8,128)(2,1)} %param.5) | copy-start | bytes 589828
  30.6 28.0 %all-to-all-start.1 = ((f32[64,16,128]{2,1,0:T(8,128)}), f32[64,16,128]{2,1,0:T(8,128)S(1)}, u32[]{:S(2)}, u32[]{:S(2)}) async-start(f32[64,16,128]{2,1,0:T(8,128)} %bitcast.63), calls=%async_computation.1 | async-start | bytes 1048576 | tf_op jit(solution)/shard_map/all_to_all | solution.py:31
  43.9 41.1 %collective-permute-start.1 = (bf16[96,4096]{1,0:T(8,128)(2,1)S(1)}, bf16[96,4096]{1,0:T(8,128)(2,1)}, u32[]{:S(2)}, u32[]{:S(2)}) collective-permute-start(bf16[96,4096]{1,0:T(8,128)(2,1)S(1)} %bitcast.57), channel_id=1, source_target_pairs={{0,7},{1,0},{2,1},{3,2},{4,3},{5,4},{6,5},{7,6},{8,15},{9,8},{10,9... | collective-permute-start | bytes 2359304 | tf_op jit(solution)/shard_map/ppermute | solution.py:143
  45.9 66.3 %copy-start.4 = (bf16[96,4096]{1,0:T(8,128)(2,1)}, bf16[96,4096]{1,0:T(8,128)(2,1)S(1)}, u32[]{:S(2)}) copy-start(bf16[96,4096]{1,0:T(8,128)(2,1)S(1)} %collective-permute-done.refs_1_) | copy-start | bytes 2359300
  45.9 41.0 %collective-permute-start.2 = (bf16[96,4096]{1,0:T(8,128)(2,1)S(1)}, bf16[96,4096]{1,0:T(8,128)(2,1)}, u32[]{:S(2)}, u32[]{:S(2)}) collective-permute-start(bf16[96,4096]{1,0:T(8,128)(2,1)S(1)} %collective-permute-done.refs_1_), channel_id=1, source_target_pairs={{0,1},{1,2},{2,3},{3,4},{4,5},{5,6},{6,7},{7,0},{8,9},{9,10},{10,1... | collective-permute-start | bytes 2359304 | tf_op jit(solution)/shard_map/ppermute | solution.py:140
  75.2 35.7 %all-to-all-start.3 = ((f32[64,16,128]{2,1,0:T(8,128)}), f32[64,16,128]{2,1,0:T(8,128)}, u32[]{:S(2)}, u32[]{:S(2)}) async-start(f32[64,16,128]{2,1,0:T(8,128)} %broadcast_in_dim.15), calls=%async_computation.3 | async-start | bytes 1048576 | tf_op jit(solution)/shard_map/all_to_all | solution.py:31
  85.0 26.0 %copy-start.8 = (bf16[768,128]{1,0:T(8,128)(2,1)}, bf16[768,128]{1,0:T(8,128)(2,1)S(1)}, u32[]{:S(2)}) copy-start(bf16[768,128]{1,0:T(8,128)(2,1)S(1)} %fusion.10) | copy-start | bytes 589828
  85.0 20.4 %collective-permute-start.3 = (bf16[96,4096]{1,0:T(8,128)(2,1)}, bf16[96,4096]{1,0:T(8,128)(2,1)}, u32[]{:S(2)}, u32[]{:S(2)}) collective-permute-start(bf16[96,4096]{1,0:T(8,128)(2,1)} %collective-permute-done.1.refs_2_), channel_id=1, source_target_pairs={{0,7},{1,0},{2,1},{3,2},{4,3},{5,4},{6,5},{7,6},{8,15},{9,8},{10,9... | collective-permute-start | bytes 2359304 | tf_op jit(solution)/shard_map/ppermute | solution.py:143
  86.9 21.4 %collective-permute-start.4 = (bf16[96,4096]{1,0:T(8,128)(2,1)}, bf16[96,4096]{1,0:T(8,128)(2,1)}, u32[]{:S(2)}, u32[]{:S(2)}) collective-permute-start(bf16[96,4096]{1,0:T(8,128)(2,1)} %collective-permute-done.2.refs_3_), channel_id=1, source_target_pairs={{0,1},{1,2},{2,3},{3,4},{4,5},{5,6},{6,7},{7,0},{8,9},{9,10},{10,1... | collective-permute-start | bytes 2359304 | tf_op jit(solution)/shard_map/ppermute | solution.py:140
  105.4 61.0 %collective-permute-start.5 = (bf16[96,4096]{1,0:T(8,128)(2,1)}, bf16[96,4096]{1,0:T(8,128)(2,1)}, u32[]{:S(2)}, u32[]{:S(2)}) collective-permute-start(bf16[96,4096]{1,0:T(8,128)(2,1)} %collective-permute-done.3.refs_4_), channel_id=1, source_target_pairs={{0,7},{1,0},{2,1},{3,2},{4,3},{5,4},{6,5},{7,6},{8,15},{9,8},{10,9... | collective-permute-start | bytes 2359304 | tf_op jit(solution)/shard_map/ppermute | solution.py:143
  108.3 58.0 %collective-permute-start.6 = (bf16[96,4096]{1,0:T(8,128)(2,1)}, bf16[96,4096]{1,0:T(8,128)(2,1)}, u32[]{:S(2)}, u32[]{:S(2)}) collective-permute-start(bf16[96,4096]{1,0:T(8,128)(2,1)} %collective-permute-done.4.refs_5_), channel_id=1, source_target_pairs={{0,1},{1,2},{2,3},{3,4},{4,5},{5,6},{6,7},{7,0},{8,9},{9,10},{10,1... | collective-permute-start | bytes 2359304 | tf_op jit(solution)/shard_map/ppermute | solution.py:140
  113.3 21.2 %copy-start.7 = (bf16[1,768,128]{2,1,0:T(8,128)(2,1)S(1)}, bf16[1,768,128]{2,1,0:T(8,128)(2,1)}, u32[]{:S(2)}) copy-start(bf16[1,768,128]{2,1,0:T(8,128)(2,1)} %param.5) | copy-start | bytes 589828
  113.7 32.1 %copy-start.9 = (bf16[768,128]{1,0:T(8,128)(2,1)S(1)}, bf16[768,128]{1,0:T(8,128)(2,1)}, u32[]{:S(2)}) copy-start(bf16[768,128]{1,0:T(8,128)(2,1)} %copy-done.8) | copy-start | bytes 589828
  121.6 12.7 %all-to-all-start.4 = ((f32[8,32,96]{2,1,0:T(8,128)}), f32[8,32,96]{2,1,0:T(8,128)S(1)}, u32[]{:S(2)}, u32[]{:S(2)}) async-start(f32[8,32,96]{2,1,0:T(8,128)} %broadcast_in_dim.16), calls=%async_computation.4 | async-start | bytes 262144 | tf_op jit(solution)/shard_map/all_to_all | solution.py:31
  135.6 22.0 %all-to-all-start.5 = ((f32[16,32,128]{2,1,0:T(8,128)}), f32[16,32,128]{2,1,0:T(8,128)S(1)}, u32[]{:S(2)}, u32[]{:S(2)}) async-start(f32[16,32,128]{2,1,0:T(8,128)} %broadcast_in_dim.17), calls=%async_computation.5 | async-start | bytes 524288 | tf_op jit(solution)/shard_map/all_to_all | solution.py:31
  158.2 16.1 %all-to-all-start.6 = ((f32[8,32,128]{2,1,0:T(8,128)}), f32[8,32,128]{2,1,0:T(8,128)S(1)}, u32[]{:S(2)}, u32[]{:S(2)}) async-start(f32[8,32,128]{2,1,0:T(8,128)} %broadcast_in_dim.18), calls=%async_computation.6 | async-start | bytes 262144 | tf_op jit(solution)/shard_map/all_to_all | solution.py:31
  166.4 1.1 copy-start.2
  167.5 1.1 copy-start.5
  174.3 1.0 copy-start.3

commit v4 on v2

--- a/solution.py
+++ b/solution.py
@@ -42,6 +42,35 @@
 def split(value):
     head = value.astype(BF16)
     return head, (value - head.astype(F32)).astype(BF16)
+
+
+def factor_body(rows, inverse):
+    value = rows[...]
+    left = lax.dot_general(value, value, (ROWS, ((), ())), precision=HIGH, preferred_element_type=F32)
+    rank = left.shape[0]
+    row = lax.broadcasted_iota(jnp.int32, (rank, rank), 0)
+    column = lax.broadcasted_iota(jnp.int32, (rank, rank), 1)
+    right = jnp.where(row == column, 1.0, 0.0).astype(F32)
+    for k in range(rank):
+        scale = lax.rsqrt(left[k : k + 1, k : k + 1])
+        upper = left[k : k + 1] * scale
+        solved = right[k : k + 1] * scale
+        if k + 1 < rank:
+            below = jnp.where(row[:, :1] > k, left[:, k : k + 1] * scale, 0.0)
+            left = left - below * upper
+            right = right - below * solved
+        right = jnp.where(row == k, solved, right)
+    inverse[...] = right
+
+
+def factor(rows):
+    rank = rows.shape[0]
+    return pl.pallas_call(
+        factor_body,
+        out_shape=jax.ShapeDtypeStruct((rank, rank), F32),
+        compiler_params=pltpu.CompilerParams(vmem_limit_bytes=8 * 2**20),
+        name="factor",
+    )(rows)
 
 
 def merge_body(inputs, grads, errors, basis, merged, q_out, turned):
@@ -121,7 +150,7 @@
             jax.ShapeDtypeStruct((rank, cols), F32),
         ],
         scratch_shapes=[pltpu.VMEM((3 * rank, cols), BF16)],
-        compiler_params=pltpu.CompilerParams(vmem_limit_bytes=24 * 2**20),
+        compiler_params=pltpu.CompilerParams(vmem_limit_bytes=52 * 2**20),
         cost_estimate=pl.CostEstimate(
             flops=6 * rank * wide * cols, bytes_accessed=6 * wide * cols, transcendentals=0
         ),
@@ -151,21 +180,17 @@
     halves = plane // columns
     depth = rank // halves
     pieces = jnp.transpose(p_local.reshape(halves, depth, columns, lanes), (0, 2, 1, 3))
-    pieces = pieces.reshape(plane, depth, lanes).astype(BF16)
-    piece = jnp.sum(swap(pieces, PLANE).astype(F32), axis=0)
+    pieces = pieces.reshape(plane, depth, lanes)
+    piece = jnp.sum(swap(pieces, PLANE), axis=0)
     piece = jnp.sum(spread(piece, ("c", "z")), axis=0)
     p_sum = spread(piece, PLANE).reshape(halves, columns, depth, lanes)
     p_sum = jnp.transpose(p_sum, (0, 2, 1, 3)).reshape(rank, wide)
 
-    gram = lax.dot_general(p_sum, p_sum, (((1,), (1,)), ((), ())), precision=HIGH)
-    lower = jnp.linalg.cholesky(gram)
-    inverse = lax.linalg.triangular_solve(lower, jnp.eye(rank, dtype=F32), left_side=True, lower=True)
-    p_basis = jnp.dot(inverse, p_sum, precision=HIGH)
-
-    merged, q_local = merge(gathered, grads, errors, p_basis, 1024)
-    q_local = q_local + lax.ppermute(q_local, "c", [(0, 1), (1, 0)])
-    q_local = jnp.sum(spread(q_local, "x"), axis=0)
-    error_next, q_mean = finish(merged, p_basis, spread(q_local, "y"), 1.0 / replicas, 2048)
+    p_basis = jnp.dot(factor(p_sum), p_sum, precision=HIGH)
+
+    merged, q_local = merge(gathered, grads, errors, p_basis, 2048)
+    q_local = jnp.sum(spread(q_local.astype(BF16), ("y", "c")).astype(F32), axis=0)
+    error_next, q_mean = finish(merged, p_basis, spread(q_local, "x"), 1.0 / replicas, 2048)
     return (error_next[None], p_basis.T, q_mean.T)
 
 

time: 157 us -> 154 us (0.981); the launches traced: 155 us -> 154 us
  blocking collectives: 111 us -> 121 us
  other arithmetic: 7.64 us -> 0.94 us
  starting transfers between devices: 4.58 us -> 0.04 us
  Pallas kernels: 7.42 us -> 10.6 us
    all_to_all x6, blocking collectives: 111 us -> 121 us  [swap(): return lax.all_to_all(value, axes, 0, 0, tiled=True)]
    another operation x5 -> x0, other arithmetic: 6.71 us -> none  [the longest x3 3.6 us: on_device(): lower = jnp.linalg.cholesky(gram)]
    ppermute x1 -> x0, starting transfers between devices: 4.54 us -> none  [on_device(): q_local = q_local + lax.ppermute(q_local, 'c', [(0, 1), (1, 0)])]
    pallas_call x0 -> x1, Pallas kernels: none -> 3.13 us  [factor(): pl.pallas_call(factor_body, out_shape=jax.ShapeDtypeStruct((rank, rank),...]
  transfers between devices with their start and end apart: 2 -> 1, of which waited for: 1 -> 0; matrix products, arithmetic and copies ran while one was open for 9% -> 5% of each run, Pallas kernels for 0% -> 2%
where the time goes in v4:
time: 154 us
  blocking collectives  121 us (79%)
  between operations  14.2 us (9%)
  Pallas kernels  10.6 us (7%)
  matrix products  5.1 us (3%)
    all_to_all x6, blocking collectives, swap(): return lax.all_to_all(value, axes, 0, 0, tiled=True)  121 us
    pallas_call x1, Pallas kernels, merge(): pl.pallas_call(merge_body, grid=(wide // block,), in_specs=[pl.BlockSpec(...  4.73 us
    pallas_call x1, Pallas kernels, factor(): pl.pallas_call(factor_body, out_shape=jax.ShapeDtypeStruct((rank, rank),...  3.13 us
  transfers between devices with their start and end apart: 1, of which 0 were waited for; matrix products, arithmetic and copies ran while one was open for 5% of the time, Pallas kernels for 2%

profile of v4, /device:TPU:1, one launch (start us, length us, event | category | flops | bytes accessed | tf_op | source)
XLA Modules:
  0.0 153.9 jit_solution(12847969153636257909)
XLA Ops:
  7.2 0.0 all-gather.3.cloned.1.call-start
  7.2 0.7 all-gather.3.cloned.1.call-update
  7.9 0.7 reduce-precision_convert_fusion.1
  8.6 1.1 fusion.8
  9.8 0.1 reshape.25
  9.9 24.8 %all_to_all.30 = f32[8,32,96]{2,1,0:T(8,128)S(1)} all-to-all(f32[8,32,96]{2,1,0:T(8,128)S(1)} %bitcast.46), channel_id=1, replica_groups=mesh['x'=8,'y'=8,'c'=2,'z'=8] {'z'}, dimensions={0} | all-to-all | bytes 196608 | tf_op jit(solution)/shard_map/all_to_all | solution.py:31
  34.7 1.4 fusion
  36.2 1.7 %convolution_add_fusion = f32[64,4096]{1,0:T(8,128)S(1)} fusion(f32[64,4096]{1,0:T(8,128)S(1)} %fusion, bf16[32,128]{1,0:T(8,128)(2,1)S(1)} %get-tuple-element.14, bf16[32,128]{1,0:T(8,128)(2,1)S(1)} %get-tuple-element.13, bf16[1,4096,128]{2,1,0:T(8,128)(2,1)} %param.6), kind=kOutput, calls=%fused_computation | convolution fusion | flops 67403776 | bytes 3162112 | tf_op jit(solution)/shard_map/dot_general | solution.py:176
  37.9 0.0 copy-start.1
  37.9 0.0 copy-start.2
  37.9 0.1 fusion.2
  38.0 0.1 copy.15
  38.1 0.3 copy.13
  38.4 28.3 %all_to_all.31 = f32[64,16,128]{2,1,0:T(8,128)S(1)} all-to-all(f32[64,16,128]{2,1,0:T(8,128)S(1)} %bitcast.44), channel_id=1, replica_groups=mesh['x'=8,'y'=8,'c'=2,'z'=8] {'x','y'}, dimensions={0} | all-to-all | bytes 1048576 | tf_op jit(solution)/shard_map/all_to_all | solution.py:31
  66.7 0.1 reduce_sum.37
  66.8 16.8 %all_to_all.32 = f32[16,16,128]{2,1,0:T(8,128)S(1)} all-to-all(f32[16,16,128]{2,1,0:T(8,128)S(1)} %broadcast_in_dim.10), channel_id=1, replica_groups=mesh['x'=8,'y'=8,'c'=2,'z'=8] {'c','z'}, dimensions={0} | all-to-all | bytes 262144 | tf_op jit(solution)/shard_map/all_to_all | solution.py:31
  83.6 21.2 %all_to_all.33 = f32[64,16,128]{2,1,0:T(8,128)S(1)} all-to-all(f32[64,16,128]{2,1,0:T(8,128)S(1)} %broadcast_in_dim.11), channel_id=1, replica_groups=mesh['x'=8,'y'=8,'c'=2,'z'=8] {'x','y'}, dimensions={0} | all-to-all | bytes 1048576 | tf_op jit(solution)/shard_map/all_to_all | solution.py:31
  104.8 0.2 copy.14
  104.9 0.3 copy.20
  105.2 3.1 %factor.1 = f32[32,32]{1,0:T(8,128)S(1)} custom-call(f32[32,4096]{1,0:T(8,128)S(1)} %bitcast.38), custom_call_target="tpu_custom_call" | custom-call | tf_op jit(solution)/shard_map/factor/pallas_call | solution.py:68
  108.4 0.9 fusion.14.basis
  109.2 0.0 copy-start
  109.3 0.0 all-gather.3.cloned.1.call-done
  109.3 0.0 copy-done.1
  109.3 0.0 copy-done.2
  109.3 4.7 %merge.1 = (f32[4096,128]{1,0:T(8,128)}, f32[32,128]{1,0:T(8,128)S(1)}) custom-call(bf16[768,4096]{1,0:T(8,128)(2,1)} %bitcast.40, bf16[768,128]{1,0:T(8,128)(2,1)S(1)} %bitcast.39, bf16[4096,128]{1,0:T(8,128)(2,1)S(1)} %bitcast.37, f32[32,4096]{1,0:T(8,128)S(1)} %fusion.14.basis), custom_call_target="tpu_custom_call" | custom-call | flops 805306368 | bytes 6291456 | tf_op jit(solution)/shard_map/merge/pallas_call | solution.py:94
  114.1 16.9 %all_to_all.34 = bf16[16,32,128]{2,1,0:T(8,128)(2,1)S(1)} all-to-all(bf16[16,32,128]{2,1,0:T(8,128)(2,1)S(1)} %broadcast_in_dim.12), channel_id=1, replica_groups=mesh['x'=8,'y'=8,'c'=2,'z'=8] {'y','c'}, dimensions={0} | all-to-all | bytes 262144 | tf_op jit(solution)/shard_map/all_to_all | solution.py:31
  131.0 13.3 %all_to_all.35.terms = f32[8,32,128]{2,1,0:T(8,128)S(1)} all-to-all(f32[8,32,128]{2,1,0:T(8,128)S(1)} %broadcast_in_dim.13), channel_id=1, replica_groups=mesh['x'=8,'y'=8,'c'=2,'z'=8] {'x'}, dimensions={0} | all-to-all | bytes 262144 | tf_op jit(solution)/shard_map/all_to_all | solution.py:31
  144.3 2.7 %finish.1 = (bf16[4096,128]{1,0:T(8,128)(2,1)}, f32[32,128]{1,0:T(8,128)}) custom-call(f32[4096,128]{1,0:T(8,128)} %get-tuple-element.7.merged, f32[32,4096]{1,0:T(8,128)S(1)} %fusion.14.basis, f32[8,32,128]{2,1,0:T(8,128)S(1)} %all_to_all.35.terms), custom_call_target="tpu_custom_call" | custom-call | flops 100663296 | bytes 3145728 | tf_op jit(solution)/shard_map/finish/pallas_call | solution.py:136
  147.1 0.0 copy-done
  (11 shorter events, 0.2 us)
Async XLA Ops:
  7.2 102.1 %all-gather.3.cloned.1.call-start = ((), (), s32[]{:S(2)}) async-start(), calls=%async_computation.6 | async-start | bytes 7077888 | tf_op jit(solution)/shard_map/all_gather | solution.py:168
  37.9 71.4 %copy-start.1 = (bf16[1,4096,128]{2,1,0:T(8,128)(2,1)S(1)}, bf16[1,4096,128]{2,1,0:T(8,128)(2,1)}, u32[]{:S(2)}) copy-start(bf16[1,4096,128]{2,1,0:T(8,128)(2,1)} %param.6) | copy-start | bytes 3145732
  37.9 71.4 %copy-start.2 = (bf16[1,768,128]{2,1,0:T(8,128)(2,1)S(1)}, bf16[1,768,128]{2,1,0:T(8,128)(2,1)}, u32[]{:S(2)}) copy-start(bf16[1,768,128]{2,1,0:T(8,128)(2,1)} %param.5) | copy-start | bytes 589828
  109.2 37.8 %copy-start = (f32[32,4096]{1,0:T(8,128)}, f32[32,4096]{1,0:T(8,128)S(1)}, u32[]{:S(2)}) copy-start(f32[32,4096]{1,0:T(8,128)S(1)} %fusion.14.basis) | copy-start | bytes 1572868
Sparse Core Ops, SparseCore 0:
  10.7 96.8 all-gather.2

commit v5 on v4

v5 whole, which is shorter than its diff:
```python
import functools
import math

import jax
import jax.numpy as jnp
from jax import lax
from jax.experimental import pallas as pl
from jax.experimental.pallas import tpu as pltpu
from jax.sharding import Mesh, PartitionSpec as P

F32 = jnp.float32
BF16 = jnp.bfloat16
HIGH = lax.Precision.HIGHEST
PLANE = ("x", "y")
ROWS = ((1,), (1,))
COLUMNS = ((0,), (0,))
PLAIN = ((1,), (0,))


def fold(value):
    half = value.shape[0] // 2
    return value[:half] + value[half:]


def swap(value, axes):
    return lax.all_to_all(value, axes, 0, 0, tiled=True)


def spread(value, axes):
    return swap(jnp.broadcast_to(value[None], (lax.axis_size(axes),) + value.shape), axes)


def dot(a, b, axes=PLAIN):
    return lax.dot_general(a, b, (axes, ((), ())), preferred_element_type=F32)


def split(value):
    head = value.astype(BF16)
    return head, (value - head.astype(F32)).astype(BF16)


def heads_body(q_turned, grads, out):
    high, low = split(q_turned[...])
    both = jnp.concatenate([high, low], axis=0)
    count, _, rows = out.shape
    for t in range(count):
        out[t] = fold(dot(both, grads[t * rows : (t + 1) * rows, :], ROWS))


def heads(q_turned, grads, count):
    rank = q_turned.shape[0]
    return pl.pallas_call(
        heads_body,
        out_shape=jax.ShapeDtypeStruct((count, rank, grads.shape[0] // count), F32),
        compiler_params=pltpu.CompilerParams(vmem_limit_bytes=56 * 2**20),
        name="heads",
    )(q_turned, grads)


def terms_body(received, q_turned, inputs, errors, out):
    high, low = split(jnp.sum(received[...], axis=0))
    met = jnp.concatenate([high, low], axis=0)
    high, low = split(q_turned[...])
    both = jnp.concatenate([high, low], axis=0)
    count, depth, lanes = out.shape
    columns = inputs.shape[1] // lanes
    wide = 8 * lanes
    for start in range(0, inputs.shape[1], wide):
        part = dot(met, inputs[:, start : start + wide]) + dot(both, errors[start : start + wide, :], ROWS)
        part = fold(part)
        for h in range(count // columns):
            for j in range(wide // lanes):
                piece = part[h * depth : (h + 1) * depth, j * lanes : (j + 1) * lanes]
                out[h * columns + start // lanes + j] = piece


def make_terms(received, q_turned, inputs, errors, count):
    rank, lanes = q_turned.shape
    depth = rank * inputs.shape[1] // (count * lanes)
    return pl.pallas_call(
        terms_body,
        out_shape=jax.ShapeDtypeStruct((count, depth, lanes), F32),
        compiler_params=pltpu.CompilerParams(vmem_limit_bytes=56 * 2**20),
        name="terms",
    )(received, q_turned, inputs, errors)


def basis_body(pieces, basis, again):
    count, depth, lanes = pieces.shape
    rank, wide = basis.shape
    columns = wide // lanes
    value = jnp.concatenate(
        [
            jnp.concatenate([pieces[h * columns + j] for j in range(columns)], axis=1)
            for h in range(count // columns)
        ],
        axis=0,
    )
    left = lax.dot_general(value, value, (ROWS, ((), ())), precision=HIGH, preferred_element_type=F32)
    row = lax.broadcasted_iota(jnp.int32, (rank, rank), 0)
    column = lax.broadcasted_iota(jnp.int32, (rank, rank), 1)
    right = jnp.where(row == column, 1.0, 0.0).astype(F32)
    for k in range(rank):
        scale = lax.rsqrt(left[k : k + 1, k : k + 1])
        upper = left[k : k + 1] * scale
        solved = right[k : k + 1] * scale
        if k + 1 < rank:
            below = jnp.where(row[:, :1] > k, left[:, k : k + 1] * scale, 0.0)
            left = left - below * upper
            right = right - below * solved
        right = jnp.where(row == k, solved, right)
    result = lax.dot_general(right, value, (PLAIN, ((), ())), precision=HIGH, preferred_element_type=F32)
    basis[...] = result
    again[...] = result


def make_basis(pieces, rank):
    count, depth, lanes = pieces.shape
    return pl.pallas_call(
        basis_body,
        out_shape=[jax.ShapeDtypeStruct((rank, count * depth * lanes // rank), F32)] * 2,
        compiler_params=pltpu.CompilerParams(vmem_limit_bytes=12 * 2**20),
        name="basis",
    )(pieces)


def merge_body(inputs, grads, errors, basis, merged, q_out, held, sems):
    count, _, block = held.shape

    def fetch(i):
        return pltpu.make_async_copy(inputs.at[:, pl.ds(i * block, block)], held.at[i], sems.at[i])

    for i in range(count):
        fetch(i).start()
    turned = grads[...].T
    b_high, b_low = split(basis[...])
    rank = b_high.shape[0]
    both = jnp.concatenate([b_high, b_low], axis=0)
    total = jnp.zeros(q_out.shape, F32)
    for i in range(count):
        here = slice(i * block, (i + 1) * block)
        fetch(i).wait()
        part = dot(turned, held[i]).T + errors[here, :].astype(F32)
        merged[here, :] = part
        high, low = split(part)
        total += fold(dot(both[:, here], high)) + dot(b_high[:, here], low)
    q_out[...] = total


def merge(inputs, grads, errors, basis, block):
    tokens, wide = inputs.shape
    cols, rank = grads.shape[1], basis.shape[0]
    count = wide // block
    vmem = pl.BlockSpec(memory_space=pltpu.VMEM)
    return pl.pallas_call(
        merge_body,
        in_specs=[pl.BlockSpec(memory_space=pltpu.HBM), vmem, vmem, vmem],
        out_specs=[vmem, vmem],
        out_shape=[
            jax.ShapeDtypeStruct((wide, cols), F32),
            jax.ShapeDtypeStruct((rank, cols), F32),
        ],
        scratch_shapes=[pltpu.VMEM((count, tokens, block), BF16), pltpu.SemaphoreType.DMA((count,))],
        compiler_params=pltpu.CompilerParams(vmem_limit_bytes=46 * 2**20),
        cost_estimate=pl.CostEstimate(
            flops=2 * tokens * wide * cols, bytes_accessed=2 * tokens * wide, transcendentals=0
        ),
        name="merge",
    )(inputs, grads, errors, basis)


def finish_body(scale, merged, basis, terms, error_next, q_mean, factors):
    @pl.when(pl.program_id(0) == 0)
    def _():
        mean = jnp.sum(terms[...].astype(F32), axis=0) * scale
        q_mean[...] = mean
        high, low = split(mean)
        factors[...] = jnp.concatenate([high, low, high], axis=0)

    high, low = split(basis[...])
    approx = dot(jnp.concatenate([high, high, low], axis=0), factors[...], COLUMNS)
    error_next[...] = (merged[...] - approx).astype(BF16)


def finish(merged, basis, terms, scale, block):
    wide, cols = merged.shape
    rank = basis.shape[0]
    return pl.pallas_call(
        functools.partial(finish_body, scale),
        grid=(wide // block,),
        in_specs=[
            pl.BlockSpec((block, cols), lambda i: (i, 0)),
            pl.BlockSpec((rank, block), lambda i: (0, i)),
            pl.BlockSpec(terms.shape, lambda i: (0, 0, 0)),
        ],
        out_specs=[
            pl.BlockSpec((block, cols), lambda i: (i, 0)),
            pl.BlockSpec((rank, cols), lambda i: (0, 0)),
        ],
        out_shape=[
            jax.ShapeDtypeStruct((wide, cols), BF16),
            jax.ShapeDtypeStruct((rank, cols), F32),
        ],
        scratch_shapes=[pltpu.VMEM((3 * rank, cols), BF16)],
        compiler_params=pltpu.CompilerParams(vmem_limit_bytes=24 * 2**20),
        cost_estimate=pl.CostEstimate(
            flops=6 * rank * wide * cols, bytes_accessed=6 * wide * cols, transcendentals=0
        ),
        name="finish",
    )(merged, basis, terms)


def on_device(normed, key_grad, error_in, q_init):
    inputs, grads, errors = normed[0], key_grad[0], error_in[0]
    tp = lax.axis_size("z")
    plane = lax.axis_size(PLANE)
    replicas = plane * lax.axis_size("c")
    rank = q_init.shape[1]
    gathered = lax.all_gather(inputs, "z", axis=0, tiled=True)

    q_turned = q_init.T
    pieces = make_terms(swap(heads(q_turned, grads, tp), "z"), q_turned, inputs, errors, plane)
    piece = jnp.sum(swap(pieces, PLANE), axis=0)
    piece = jnp.sum(spread(piece, ("c", "z")), axis=0)
    p_basis, basis = make_basis(spread(piece, PLANE), rank)

    merged, q_local = merge(gathered, grads, errors, basis, 2048)
    q_local = jnp.sum(spread(q_local.astype(BF16), ("y", "c")).astype(F32), axis=0)
    q_local = lax.optimization_barrier(q_local).astype(BF16)
    error_next, q_mean = finish(merged, basis, spread(q_local, "x"), 1.0 / replicas, 2048)
    return (error_next[None], p_basis.T, q_mean.T)


def solution(mesh):
    side = math.isqrt(mesh.shape["dp"] // 2)
    whole = Mesh(mesh.devices.reshape(side, side, 2, mesh.shape["tp"]), ("x", "y", "c", "z"))
    dp = ("x", "y", "c")
    placed = (P(dp, "z", None), P(dp, None, "z"), P(dp, None, "z"), P("z", None))
    return jax.shard_map(
        on_device,
        mesh=whole,
        in_specs=placed,
        out_specs=(P(dp, None, "z"), P(), P("z", None)),
        check_vma=False,
    )
```

time: 154 us -> 150 us (0.974)
  matrix products: 5.1 us -> 0 us
  Pallas kernels: 10.6 us -> 15.4 us
  blocking collectives: 121 us -> 119 us
    pallas_call x2 -> x4, Pallas kernels: 7.86 us -> 13.8 us  [the longest x1 5.23 us: make_basis(): pl.pallas_call(basis_body, out_shape=[jax.ShapeDtypeStruct((rank, count *...]
    dot_general x4 -> x0, matrix products: 5.1 us -> none  [the longest x1 1.7 us: on_device(): lax.dot_general(q_terms, errors, (((1,), (1,)), ((), ())), preferred_elem...]
    all_to_all x6, blocking collectives: 121 us -> 119 us  [swap(): return lax.all_to_all(value, axes, 0, 0, tiled=True)]
  transfers between devices with their start and end apart: 1 -> 1, of which waited for: 0 -> 0; matrix products, arithmetic and copies ran while one was open for 5% -> 0% of each run, Pallas kernels for 2% -> 7%
where the time goes in v5:
time: 150 us
  blocking collectives  119 us (79%)
  Pallas kernels  15.4 us (10%)
  between operations  14.1 us (9%)
    all_to_all x6, blocking collectives, swap(): return lax.all_to_all(value, axes, 0, 0, tiled=True)  119 us
    pallas_call x1, Pallas kernels, make_basis(): pl.pallas_call(basis_body, out_shape=[jax.ShapeDtypeStruct((rank, count *...  5.23 us
    pallas_call x1, Pallas kernels, merge(): pl.pallas_call(merge_body, in_specs=[pl.BlockSpec(memory_space=pltpu.HBM)...  3.77 us
  transfers between devices with their start and end apart: 1, of which 0 were waited for; matrix products, arithmetic and copies ran while one was open for 0% of the time, Pallas kernels for 7%

profile of v5, /device:TPU:1, one launch (start us, length us, event | category | flops | bytes accessed | tf_op | source)
XLA Modules:
  0.0 149.9 jit_solution(7635655702639849497)
XLA Ops:
  7.2 0.0 copy-start.1
  7.2 0.0 copy-start
  7.2 0.0 all-gather.3.cloned.1.call-start
  7.2 0.7 all-gather.3.cloned.1.call-update
  7.9 1.8 %heads.1 = f32[8,32,96]{2,1,0:T(8,128)} custom-call(f32[32,128]{1,0:T(8,128)} %bitcast.14, bf16[768,128]{1,0:T(8,128)(2,1)} %bitcast.10), custom_call_target="tpu_custom_call" | custom-call | tf_op jit(solution)/shard_map/heads/pallas_call | solution.py:52
  9.8 25.1 %all_to_all.30.received = f32[8,32,96]{2,1,0:T(8,128)} all-to-all(f32[8,32,96]{2,1,0:T(8,128)} %heads.1), channel_id=1, replica_groups=mesh['x'=8,'y'=8,'c'=2,'z'=8] {'z'}, dimensions={0} | all-to-all | bytes 196608 | tf_op jit(solution)/shard_map/all_to_all | solution.py:26
  34.9 3.0 %terms.1 = f32[64,16,128]{2,1,0:T(8,128)} custom-call(f32[8,32,96]{2,1,0:T(8,128)} %all_to_all.30.received, f32[32,128]{1,0:T(8,128)} %bitcast.15, bf16[96,4096]{1,0:T(8,128)(2,1)} %bitcast.13, bf16[4096,128]{1,0:T(8,128)(2,1)} %bitcast.8), custom_call_target="tpu_custom_call" | custom-call | tf_op jit(solution)/shard_map/terms/pallas_call | solution.py:80
  37.9 28.6 %all_to_all.31 = f32[64,16,128]{2,1,0:T(8,128)S(1)} all-to-all(f32[64,16,128]{2,1,0:T(8,128)} %terms.1), channel_id=1, replica_groups=mesh['x'=8,'y'=8,'c'=2,'z'=8] {'x','y'}, dimensions={0} | all-to-all | bytes 1048576 | tf_op jit(solution)/shard_map/all_to_all | solution.py:26
  66.4 0.1 reduce_sum.27
  66.5 16.7 %all_to_all.32 = f32[16,16,128]{2,1,0:T(8,128)S(1)} all-to-all(f32[16,16,128]{2,1,0:T(8,128)S(1)} %broadcast_in_dim.10), channel_id=1, replica_groups=mesh['x'=8,'y'=8,'c'=2,'z'=8] {'c','z'}, dimensions={0} | all-to-all | bytes 262144 | tf_op jit(solution)/shard_map/all_to_all | solution.py:26
  83.2 21.2 %all_to_all.33.pieces = f32[64,16,128]{2,1,0:T(8,128)S(1)} all-to-all(f32[64,16,128]{2,1,0:T(8,128)S(1)} %broadcast_in_dim.11), channel_id=1, replica_groups=mesh['x'=8,'y'=8,'c'=2,'z'=8] {'x','y'}, dimensions={0} | all-to-all | bytes 1048576 | tf_op jit(solution)/shard_map/all_to_all | solution.py:26
  104.4 5.2 %basis.1 = (f32[32,4096]{1,0:T(8,128)}, f32[32,4096]{1,0:T(8,128)S(1)}) custom-call(f32[64,16,128]{2,1,0:T(8,128)S(1)} %all_to_all.33.pieces), custom_call_target="tpu_custom_call" | custom-call | tf_op jit(solution)/shard_map/basis/pallas_call | solution.py:119
  109.7 0.0 all-gather.3.cloned.1.call-done
  109.7 0.0 copy-done.1
  109.7 0.0 copy-done
  109.7 3.8 %merge.1 = (f32[4096,128]{1,0:T(8,128)S(1)}, f32[32,128]{1,0:T(8,128)S(1)}) custom-call(bf16[768,4096]{1,0:T(8,128)(2,1)} %bitcast.12, bf16[768,128]{1,0:T(8,128)(2,1)S(1)} %bitcast.11, bf16[4096,128]{1,0:T(8,128)(2,1)S(1)} %bitcast.9, f32[32,4096]{1,0:T(8,128)S(1)} %get-tuple-element.9.basis), custom_call_target="tpu_custom_call" | custom-call | flops 805306368 | bytes 6291456 | tf_op jit(solution)/shard_map/merge/pallas_call | solution.py:155
  113.5 16.9 %all_to_all.34 = bf16[16,32,128]{2,1,0:T(8,128)(2,1)S(1)} all-to-all(bf16[16,32,128]{2,1,0:T(8,128)(2,1)S(1)} %broadcast_in_dim.12), channel_id=1, replica_groups=mesh['x'=8,'y'=8,'c'=2,'z'=8] {'y','c'}, dimensions={0} | all-to-all | bytes 262144 | tf_op jit(solution)/shard_map/all_to_all | solution.py:26
  130.4 11.1 %all_to_all.35.terms = bf16[8,32,128]{2,1,0:T(8,128)(2,1)S(1)} all-to-all(bf16[8,32,128]{2,1,0:T(8,128)(2,1)S(1)} %broadcast_in_dim.13), channel_id=1, replica_groups=mesh['x'=8,'y'=8,'c'=2,'z'=8] {'x'}, dimensions={0} | all-to-all | bytes 131072 | tf_op jit(solution)/shard_map/all_to_all | solution.py:26
  141.4 1.6 %finish.1 = (bf16[4096,128]{1,0:T(8,128)(2,1)}, f32[32,128]{1,0:T(8,128)}) custom-call(f32[4096,128]{1,0:T(8,128)S(1)} %get-tuple-element.10.merged, f32[32,4096]{1,0:T(8,128)S(1)} %get-tuple-element.9.basis, bf16[8,32,128]{2,1,0:T(8,128)(2,1)S(1)} %all_to_all.35.terms), custom_call_target="tpu_custom_call" | custom-call | flops 100663296 | bytes 3145728 | tf_op jit(solution)/shard_map/finish/pallas_call | solution.py:188
  (7 shorter events, 0.1 us)
Async XLA Ops:
  7.2 102.5 %copy-start.1 = (bf16[1,768,128]{2,1,0:T(8,128)(2,1)S(1)}, bf16[1,768,128]{2,1,0:T(8,128)(2,1)}, u32[]{:S(2)}) copy-start(bf16[1,768,128]{2,1,0:T(8,128)(2,1)} %param.5) | copy-start | bytes 589828
  7.2 102.5 %copy-start = (bf16[1,4096,128]{2,1,0:T(8,128)(2,1)S(1)}, bf16[1,4096,128]{2,1,0:T(8,128)(2,1)}, u32[]{:S(2)}) copy-start(bf16[1,4096,128]{2,1,0:T(8,128)(2,1)} %param.6) | copy-start | bytes 3145732
  7.2 102.5 %all-gather.3.cloned.1.call-start = ((), (), s32[]{:S(2)}) async-start(), calls=%async_computation.6 | async-start | bytes 7077888 | tf_op jit(solution)/shard_map/all_gather | solution.py:219
Sparse Core Ops, SparseCore 0:
  10.7 96.8 all-gather.2

commit v6 on v5

--- a/solution.py
+++ b/solution.py
@@ -39,7 +39,8 @@
     return head, (value - head.astype(F32)).astype(BF16)
 
 
-def heads_body(q_turned, grads, out):
+def heads_body(q_turned, grads, side, out, passed):
+    passed[...] = side[...]
     high, low = split(q_turned[...])
     both = jnp.concatenate([high, low], axis=0)
     count, _, rows = out.shape
@@ -47,22 +48,26 @@
         out[t] = fold(dot(both, grads[t * rows : (t + 1) * rows, :], ROWS))
 
 
-def heads(q_turned, grads, count):
+def heads(q_turned, grads, side, count):
     rank = q_turned.shape[0]
     return pl.pallas_call(
         heads_body,
-        out_shape=jax.ShapeDtypeStruct((count, rank, grads.shape[0] // count), F32),
+        out_shape=[
+            jax.ShapeDtypeStruct((count, rank, grads.shape[0] // count), F32),
+            jax.ShapeDtypeStruct(side.shape, F32),
+        ],
         compiler_params=pltpu.CompilerParams(vmem_limit_bytes=56 * 2**20),
         name="heads",
-    )(q_turned, grads)
-
-
-def terms_body(received, q_turned, inputs, errors, out):
+    )(q_turned, grads, side)
+
+
+def terms_body(received, q_turned, inputs, errors, side, kept, given):
     high, low = split(jnp.sum(received[...], axis=0))
     met = jnp.concatenate([high, low], axis=0)
     high, low = split(q_turned[...])
     both = jnp.concatenate([high, low], axis=0)
-    count, depth, lanes = out.shape
+    count, depth, lanes = kept.shape
+    first = side[...] == 0.0
     columns = inputs.shape[1] // lanes
     wide = 8 * lanes
     for start in range(0, inputs.shape[1], wide):
@@ -70,29 +75,35 @@
         part = fold(part)
         for h in range(count // columns):
             for j in range(wide // lanes):
-                piece = part[h * depth : (h + 1) * depth, j * lanes : (j + 1) * lanes]
-                out[h * columns + start // lanes + j] = piece
-
-
-def make_terms(received, q_turned, inputs, errors, count):
+                piece = part[2 * h * depth : 2 * (h + 1) * depth, j * lanes : (j + 1) * lanes]
+                place = h * columns + start // lanes + j
+                kept[place] = jnp.where(first, piece[:depth], piece[depth:])
+                given[place] = jnp.where(first, piece[depth:], piece[:depth])
+
+
+def make_terms(received, q_turned, inputs, errors, side, count):
     rank, lanes = q_turned.shape
-    depth = rank * inputs.shape[1] // (count * lanes)
+    depth = rank * inputs.shape[1] // (2 * count * lanes)
     return pl.pallas_call(
         terms_body,
-        out_shape=jax.ShapeDtypeStruct((count, depth, lanes), F32),
+        out_shape=[jax.ShapeDtypeStruct((count, depth, lanes), F32)] * 2,
         compiler_params=pltpu.CompilerParams(vmem_limit_bytes=56 * 2**20),
         name="terms",
-    )(received, q_turned, inputs, errors)
-
-
-def basis_body(pieces, basis, again):
-    count, depth, lanes = pieces.shape
+    )(received, q_turned, inputs, errors, side)
+
+
+def basis_body(own, other, side, basis, again):
+    count, _, lanes = own.shape
     rank, wide = basis.shape
+    first = side[...] == 0.0
+    upper = [jnp.where(first, own[i], other[i]) for i in range(count)]
+    lower = [jnp.where(first, other[i], own[i]) for i in range(count)]
     columns = wide // lanes
     value = jnp.concatenate(
         [
-            jnp.concatenate([pieces[h * columns + j] for j in range(columns)], axis=1)
+            jnp.concatenate([half[h * columns + j] for j in range(columns)], axis=1)
             for h in range(count // columns)
+            for half in (upper, lower)
         ],
         axis=0,
     )
@@ -114,14 +125,14 @@
     again[...] = result
 
 
-def make_basis(pieces, rank):
-    count, depth, lanes = pieces.shape
+def make_basis(own, other, side, rank):
+    wide = 2 * own.size // rank
     return pl.pallas_call(
         basis_body,
-        out_shape=[jax.ShapeDtypeStruct((rank, count * depth * lanes // rank), F32)] * 2,
+        out_shape=[jax.ShapeDtypeStruct((rank, wide), F32)] * 2,
         compiler_params=pltpu.CompilerParams(vmem_limit_bytes=12 * 2**20),
         name="basis",
-    )(pieces)
+    )(own, other, side)
 
 
 def merge_body(inputs, grads, errors, basis, merged, q_out, held, sems):
@@ -219,10 +230,14 @@
     gathered = lax.all_gather(inputs, "z", axis=0, tiled=True)
 
     q_turned = q_init.T
-    pieces = make_terms(swap(heads(q_turned, grads, tp), "z"), q_turned, inputs, errors, plane)
-    piece = jnp.sum(swap(pieces, PLANE), axis=0)
-    piece = jnp.sum(spread(piece, ("c", "z")), axis=0)
-    p_basis, basis = make_basis(spread(piece, PLANE), rank)
+    side = jnp.full((8, 128), lax.axis_index("c").astype(F32))
+    by_token, side = heads(q_turned, grads, side, tp)
+    kept, given = make_terms(swap(by_token, "z"), q_turned, inputs, errors, side, plane)
+    cross = [(0, 1), (1, 0)]
+    piece = jnp.sum(swap(kept + lax.ppermute(given, "c", cross), PLANE), axis=0)
+    piece = jnp.sum(spread(piece, "z"), axis=0)
+    half = spread(piece, PLANE)
+    p_basis, basis = make_basis(half, lax.ppermute(half, "c", cross), side, rank)
 
     merged, q_local = merge(gathered, grads, errors, basis, 2048)
     q_local = jnp.sum(spread(q_local.astype(BF16), ("y", "c")).astype(F32), axis=0)

time: 150 us -> 148 us (0.987)
  blocking collectives: 119 us -> 103 us
  starting transfers between devices: 0.04 us -> 9.73 us
  waiting for transfers between devices: 0.68 us -> 3.17 us
    all_to_all x6, blocking collectives: 119 us -> 103 us  [swap(): return lax.all_to_all(value, axes, 0, 0, tiled=True)]
    ppermute x0 -> x2, starting transfers between devices: none -> 9.7 us  [the longest x1 5.52 us: on_device(): lax.ppermute(half, 'c', cross)]
    ppermute x0 -> x2, waiting for transfers between devices: none -> 2.49 us  [the longest x1 1.35 us: on_device(): piece = jnp.sum(swap(kept + lax.ppermute(given, 'c', cross), PLANE), axis=0)]
  transfers between devices with their start and end apart: 1 -> 3, of which waited for: 0 -> 2; matrix products, arithmetic and copies ran while one was open for 0% -> 1% of each run, Pallas kernels for 7% -> 7%
where the time goes in v6:
time: 148 us
  blocking collectives  103 us (70%)
  Pallas kernels  15.3 us (10%)
  between operations  14.1 us (10%)
  starting transfers between devices  9.73 us (7%)
  waiting for transfers between devices  3.17 us (2%)
    all_to_all x6, blocking collectives, swap(): return lax.all_to_all(value, axes, 0, 0, tiled=True)  103 us
    ppermute x1, starting transfers between devices, on_device(): lax.ppermute(half, 'c', cross)  5.52 us
    pallas_call x1, Pallas kernels, make_basis(): pl.pallas_call(basis_body, out_shape=[jax.ShapeDtypeStruct((rank, wide),...  5.23 us
    ppermute x1, starting transfers between devices, on_device(): piece = jnp.sum(swap(kept + lax.ppermute(given, 'c', cross), PLANE), axis=0)  4.17 us
    pallas_call x1, Pallas kernels, merge(): pl.pallas_call(merge_body, in_specs=[pl.BlockSpec(memory_space=pltpu.HBM)...  3.77 us
  transfers between devices with their start and end apart: 3, of which 2 were waited for; matrix products, arithmetic and copies ran while one was open for 1% of the time, Pallas kernels for 7%

profile of v6, /device:TPU:1, one launch (start us, length us, event | category | flops | bytes accessed | tf_op | source)
XLA Modules:
  0.0 147.8 jit_solution(15653480931838940483)
XLA Ops:
  7.2 0.0 copy-start.1
  7.2 0.0 copy-start
  7.2 0.0 all-gather.3.cloned.1.call-start
  7.2 0.7 all-gather.3.cloned.1.call-update
  7.9 0.6 broadcast_in_dim.12.side
  8.5 1.8 %heads.1 = (f32[8,32,96]{2,1,0:T(8,128)}, f32[8,128]{1,0:T(8,128)}) custom-call(f32[32,128]{1,0:T(8,128)} %bitcast.14, bf16[768,128]{1,0:T(8,128)(2,1)} %bitcast.10, f32[8,128]{1,0:T(8,128)} %broadcast_in_dim.12.side), custom_call_target="tpu_custom_call" | custom-call | tf_op jit(solution)/shard_map/heads/pallas_call | solution.py:53
  10.3 25.1 %all_to_all.30.received = f32[8,32,96]{2,1,0:T(8,128)} all-to-all(f32[8,32,96]{2,1,0:T(8,128)} %get-tuple-element.13), channel_id=1, replica_groups=mesh['x'=8,'y'=8,'c'=2,'z'=8] {'z'}, dimensions={0} | all-to-all | bytes 196608 | tf_op jit(solution)/shard_map/all_to_all | solution.py:26
  35.4 3.0 %terms.1 = (f32[64,8,128]{2,1,0:T(8,128)}, f32[64,8,128]{2,1,0:T(8,128)}) custom-call(f32[8,32,96]{2,1,0:T(8,128)} %all_to_all.30.received, f32[32,128]{1,0:T(8,128)} %bitcast.15, bf16[96,4096]{1,0:T(8,128)(2,1)} %bitcast.13, bf16[4096,128]{1,0:T(8,128)(2,1)} %bitcast.8, f32[8,128]{1,0:T(8,128)} %get-tuple-element.14.side), custom_call_target="tpu_custom_call" | custom-call | tf_op jit(solution)/shard_map/terms/pallas_call | solution.py:87
  38.4 4.2 %collective-permute-start = (f32[64,8,128]{2,1,0:T(8,128)}, f32[64,8,128]{2,1,0:T(8,128)S(1)}, u32[]{:S(2)}, u32[]{:S(2)}) collective-permute-start(f32[64,8,128]{2,1,0:T(8,128)} %get-tuple-element.16), channel_id=1, source_target_pairs={{0,8},{8,0},{1,9},{9,1},{2,10},{10,2},{3,11},{11,3},{4,12},{12,4},... | collective-permute-start | bytes 786440 | tf_op jit(solution)/shard_map/ppermute | solution.py:237
  42.6 1.4 collective-permute-done
  43.9 1.0 add.3
  44.9 26.0 %all_to_all.31 = f32[64,8,128]{2,1,0:T(8,128)S(1)} all-to-all(f32[64,8,128]{2,1,0:T(8,128)S(1)} %add.3), channel_id=1, replica_groups=mesh['x'=8,'y'=8,'c'=2,'z'=8] {'x','y'}, dimensions={0} | all-to-all | bytes 524288 | tf_op jit(solution)/shard_map/all_to_all | solution.py:26
  70.9 0.1 reduce_sum.27
  71.0 9.6 %all_to_all.32 = f32[8,8,128]{2,1,0:T(8,128)S(1)} all-to-all(f32[8,8,128]{2,1,0:T(8,128)S(1)} %broadcast_in_dim.13), channel_id=1, replica_groups=mesh['x'=8,'y'=8,'c'=2,'z'=8] {'z'}, dimensions={0} | all-to-all | bytes 65536 | tf_op jit(solution)/shard_map/all_to_all | solution.py:26
  80.6 18.0 %all_to_all.33.own = f32[64,8,128]{2,1,0:T(8,128)S(1)} all-to-all(f32[64,8,128]{2,1,0:T(8,128)S(1)} %broadcast_in_dim.14), channel_id=1, replica_groups=mesh['x'=8,'y'=8,'c'=2,'z'=8] {'x','y'}, dimensions={0} | all-to-all | bytes 524288 | tf_op jit(solution)/shard_map/all_to_all | solution.py:26
  98.6 5.5 %collective-permute-start.1 = (f32[64,8,128]{2,1,0:T(8,128)S(1)}, f32[64,8,128]{2,1,0:T(8,128)S(1)}, u32[]{:S(2)}, u32[]{:S(2)}) collective-permute-start(f32[64,8,128]{2,1,0:T(8,128)S(1)} %all_to_all.33.own), channel_id=1, source_target_pairs={{0,8},{8,0},{1,9},{9,1},{2,10},{10,2},{3,11},{11,3},{4,12},{12,4},... | collective-permute-start | bytes 786440 | tf_op jit(solution)/shard_map/ppermute | solution.py:240
  104.1 1.1 collective-permute-done.1.other
  105.3 0.0 copy-start.2
  105.3 0.7 copy-done.2
  106.0 5.2 %basis.1 = (f32[32,4096]{1,0:T(8,128)}, f32[32,4096]{1,0:T(8,128)S(1)}) custom-call(f32[64,8,128]{2,1,0:T(8,128)S(1)} %all_to_all.33.own, f32[64,8,128]{2,1,0:T(8,128)S(1)} %collective-permute-done.1.other, f32[8,128]{1,0:T(8,128)S(1)} %copy-done.2), custom_call_target="tpu_custom_call" | custom-call | tf_op jit(solution)/shard_map/basis/pallas_call | solution.py:130
  111.2 0.0 all-gather.3.cloned.1.call-done
  111.2 0.0 copy-done.1
  111.2 0.0 copy-done
  111.2 3.8 %merge.1 = (f32[4096,128]{1,0:T(8,128)S(1)}, f32[32,128]{1,0:T(8,128)S(1)}) custom-call(bf16[768,4096]{1,0:T(8,128)(2,1)} %bitcast.12, bf16[768,128]{1,0:T(8,128)(2,1)S(1)} %bitcast.11, bf16[4096,128]{1,0:T(8,128)(2,1)S(1)} %bitcast.9, f32[32,4096]{1,0:T(8,128)S(1)} %get-tuple-element.17.basis), custom_call_target="tpu_custom_call" | custom-call | flops 805306368 | bytes 6291456 | tf_op jit(solution)/shard_map/merge/pallas_call | solution.py:166
  115.0 12.0 %all_to_all.34 = bf16[16,32,128]{2,1,0:T(8,128)(2,1)S(1)} all-to-all(bf16[16,32,128]{2,1,0:T(8,128)(2,1)S(1)} %broadcast_in_dim.15), channel_id=1, replica_groups=mesh['x'=8,'y'=8,'c'=2,'z'=8] {'y','c'}, dimensions={0} | all-to-all | bytes 262144 | tf_op jit(solution)/shard_map/all_to_all | solution.py:26
  127.1 12.3 %all_to_all.35.terms = bf16[8,32,128]{2,1,0:T(8,128)(2,1)S(1)} all-to-all(bf16[8,32,128]{2,1,0:T(8,128)(2,1)S(1)} %broadcast_in_dim.16), channel_id=1, replica_groups=mesh['x'=8,'y'=8,'c'=2,'z'=8] {'x'}, dimensions={0} | all-to-all | bytes 131072 | tf_op jit(solution)/shard_map/all_to_all | solution.py:26
  139.3 1.6 %finish.1 = (bf16[4096,128]{1,0:T(8,128)(2,1)}, f32[32,128]{1,0:T(8,128)}) custom-call(f32[4096,128]{1,0:T(8,128)S(1)} %get-tuple-element.18.merged, f32[32,4096]{1,0:T(8,128)S(1)} %get-tuple-element.17.basis, bf16[8,32,128]{2,1,0:T(8,128)(2,1)S(1)} %all_to_all.35.terms), custom_call_target="tpu_custom_call" | custom-call | flops 100663296 | bytes 3145728 | tf_op jit(solution)/shard_map/finish/pallas_call | solution.py:199
  (7 shorter events, 0.1 us)
Async XLA Ops:
  7.2 104.0 %copy-start.1 = (bf16[1,768,128]{2,1,0:T(8,128)(2,1)S(1)}, bf16[1,768,128]{2,1,0:T(8,128)(2,1)}, u32[]{:S(2)}) copy-start(bf16[1,768,128]{2,1,0:T(8,128)(2,1)} %param.5) | copy-start | bytes 589828
  7.2 104.0 %copy-start = (bf16[1,4096,128]{2,1,0:T(8,128)(2,1)S(1)}, bf16[1,4096,128]{2,1,0:T(8,128)(2,1)}, u32[]{:S(2)}) copy-start(bf16[1,4096,128]{2,1,0:T(8,128)(2,1)} %param.6) | copy-start | bytes 3145732
  7.2 104.0 %all-gather.3.cloned.1.call-start = ((), (), s32[]{:S(2)}) async-start(), calls=%async_computation.6 | async-start | bytes 7077888 | tf_op jit(solution)/shard_map/all_gather | solution.py:230
  38.4 5.5 %collective-permute-start = (f32[64,8,128]{2,1,0:T(8,128)}, f32[64,8,128]{2,1,0:T(8,128)S(1)}, u32[]{:S(2)}, u32[]{:S(2)}) collective-permute-start(f32[64,8,128]{2,1,0:T(8,128)} %get-tuple-element.16), channel_id=1, source_target_pairs={{0,8},{8,0},{1,9},{9,1},{2,10},{10,2},{3,11},{11,3},{4,12},{12,4},... | collective-permute-start | bytes 786440 | tf_op jit(solution)/shard_map/ppermute | solution.py:237
  98.6 6.7 %collective-permute-start.1 = (f32[64,8,128]{2,1,0:T(8,128)S(1)}, f32[64,8,128]{2,1,0:T(8,128)S(1)}, u32[]{:S(2)}, u32[]{:S(2)}) collective-permute-start(f32[64,8,128]{2,1,0:T(8,128)S(1)} %all_to_all.33.own), channel_id=1, source_target_pairs={{0,8},{8,0},{1,9},{9,1},{2,10},{10,2},{3,11},{11,3},{4,12},{12,4},... | collective-permute-start | bytes 786440 | tf_op jit(solution)/shard_map/ppermute | solution.py:240
  105.3 0.7 copy-start.2
Sparse Core Ops, SparseCore 0:
  10.7 94.6 all-gather.2
